TPU v7x, 128 devices: a whole 4x4x4 slice. The times are simulated.
128 devices in a mesh: section: 2 (over core), dp: 64 (over x, y, z).
Axes of the slice: x: 4, y: 4, z: 4, core: 2. Of those that a mesh axis runs over, the one named last changes fastest.
Arguments:
- boundary: bfloat16 [2, 2, 8192, 960], P('section', None, 'dp'), may hold values from -6 to 6
- lengths: int32 [2, 64], P(None, 'dp'), may hold values from 32 to 128, as said below
- gain_attn: bfloat16 [2, 960], P('section', 'dp'), may hold values from 0.099609375 to 1.8984375
- w_query: bfloat16 [2, 960, 960], P('section', 'dp'), may hold values from -0.1875 to 0.1875
- w_key: bfloat16 [2, 960, 320], P('section', 'dp'), may hold values from -0.1875 to 0.1875
- w_value: bfloat16 [2, 960, 320], P('section', 'dp'), may hold values from -0.1875 to 0.1875
- w_out: bfloat16 [2, 960, 960], P('section', None, 'dp'), may hold values from -1.5 to 1.5
- gain_mlp: bfloat16 [2, 960], P('section', 'dp'), may hold values from 0.099609375 to 1.8984375
- w_gate: bfloat16 [2, 960, 2560], P('section', 'dp'), may hold values from -0.1875 to 0.1875
- w_up: bfloat16 [2, 960, 2560], P('section', 'dp'), may hold values from -0.1875 to 0.1875
- w_down: bfloat16 [2, 2560, 960], P('section', None, 'dp'), may hold values from -0.125 to 0.125
Outputs:
- ends_out: float32 [2, 2, 8192, 960], P('section', None, 'dp')
- grad_gain_attn: float32 [2, 960], P('section', 'dp')
- grad_w_query: float32 [2, 960, 960], P('section', 'dp')
- grad_w_key: float32 [2, 960, 320], P('section', 'dp')
- grad_w_value: float32 [2, 960, 320], P('section', 'dp')
- grad_w_out: float32 [2, 960, 960], P('section', None, 'dp')
- grad_gain_mlp: float32 [2, 960], P('section', 'dp')
- grad_w_gate: float32 [2, 960, 2560], P('section', 'dp')
- grad_w_up: float32 [2, 960, 2560], P('section', 'dp')
- grad_w_down: float32 [2, 2560, 960], P('section', None, 'dp')
Inputs may be any that keep to these rules, and one draw needn't show every extreme that they name: lengths[m, s] is the number of valid leading tokens of sequence s of micro-batch m; each micro-batch has at least one sequence of full length 128.
All inputs are finite; a program needn't handle non-finite values.
Results may differ from a plain program's by a relative error of at most 0.03.
Values may be sent and summed in bfloat16 or wider, within the bound.
A program may use at most 256 MiB of HBM per device.

v0:
```python
import jax
import jax.numpy as jnp
from jax import lax
from jax.sharding import PartitionSpec as P

HQ = 15
KV = 5
HD = 64


EPS = 1e-05
NEG = -1e30
BASE = 10000.0
LOWTYPE = jnp.bfloat16
WIDETYPE = jnp.float32


def turned_gather(arrays, axis, dims):
    turned = [jnp.moveaxis(a, dim, 0) for a, dim in zip(arrays, dims)]
    widths = [t[0].size for t in turned]
    both = jnp.concatenate([t.reshape(-1, w) for t, w in zip(turned, widths)], axis=1)
    whole = lax.all_gather(both, axis, axis=0, tiled=True)
    blocks = jnp.split(whole, [sum(widths[:k]) for k in range(1, len(widths))], axis=1)
    return tuple(
        (
            jnp.moveaxis(b.reshape(-1, *t.shape[1:]), 0, dim)
            for b, t, dim in zip(blocks, turned, dims)
        )
    )


def from_behind(value, axis, steps):
    count = lax.axis_size(axis)
    leading, last = (max(0, -steps), min(count, count - steps))
    return lax.ppermute(value, axis, [(source, source + steps) for source in range(leading, last)])


def tables(seq_len):
    halfway = HD // 2
    frequency = BASE ** (-(jnp.arange(halfway, dtype=WIDETYPE) * 2.0 / HD))
    angles = jnp.arange(seq_len, dtype=WIDETYPE)[:, None] * frequency[None, :]
    return (jnp.cos(angles), jnp.sin(angles))


def rotate(vectors, cosine_table, sine_table):
    halfway = vectors.shape[-1] // 2
    first_half = vectors[..., :halfway]
    second_half = vectors[..., halfway:]
    cosine_cols = cosine_table[:, None, :]
    sine_cols = sine_table[:, None, :]
    return jnp.concatenate(
        [
            first_half * cosine_cols - second_half * sine_cols,
            second_half * cosine_cols + first_half * sine_cols,
        ],
        axis=-1,
    )


def rms_scale(matrix, gain):
    return matrix * lax.rsqrt(jnp.mean(matrix * matrix, axis=-1, keepdims=True) + EPS) * gain


def matmul(left, right):
    return jnp.dot(left, right, preferred_element_type=WIDETYPE)


def times_t(left, right):
    return lax.dot_general(left, right, (((1,), (1,)), ((), ())), preferred_element_type=WIDETYPE)


def t_times(left, right):
    return lax.dot_general(left, right, (((0,), (0,)), ((), ())), preferred_element_type=WIDETYPE)


def score_block(query_block, start, keys, length):
    block_rows = query_block.shape[0]
    scores = jnp.einsum(
        "ihgd,jhd->hgij", query_block, keys, preferred_element_type=WIDETYPE
    ) * HD ** (-0.5)
    row_pos = start + jnp.arange(block_rows, dtype=jnp.int32)[:, None]
    col_pos = jnp.arange(keys.shape[0], dtype=jnp.int32)[None, :]
    allowed = (col_pos <= row_pos) & (col_pos < length)
    return jnp.where(allowed, scores, NEG)


def attend_forward(queries, keys, values, length):
    seq_len = queries.shape[0]
    block = min(seq_len, 512)
    count = seq_len // block
    grouped = queries.reshape(count, block, KV, HQ // KV, HD)
    starts = jnp.arange(count, dtype=jnp.int32) * block

    def one_block(item):
        query_block, start = item
        masked = score_block(query_block, start, keys, length)
        highest = jnp.max(masked, axis=-1, keepdims=True)
        expos = jnp.exp(masked - highest)
        totals = jnp.sum(expos, axis=-1, keepdims=True)
        probs = (expos / totals).astype(LOWTYPE)
        mixed = jnp.einsum("hgij,jhd->ihgd", probs, values, preferred_element_type=WIDETYPE)
        return (mixed.astype(LOWTYPE), (highest + jnp.log(totals))[..., 0])

    mixed, logsum = lax.map(one_block, (grouped, starts))
    return (mixed.reshape(seq_len, HQ * HD), logsum)


def attend_backward(queries, keys, values, logsum, grad_mixed, length):
    seq_len = queries.shape[0]
    block = min(seq_len, 512)
    count = seq_len // block
    grouped = queries.reshape(count, block, KV, HQ // KV, HD)
    grad_grouped = grad_mixed.reshape(count, block, KV, HQ // KV, HD)
    starts = jnp.arange(count, dtype=jnp.int32) * block

    def one_block(carry, item):
        grad_keys, grad_values = carry
        query_block, grad_block, block_sum, start = item
        masked = score_block(query_block, start, keys, length)
        probs = jnp.exp(masked - block_sum[..., None])
        grad_probs = jnp.einsum(
            "ihgd,jhd->hgij", grad_block, values, preferred_element_type=WIDETYPE
        )
        inner = jnp.sum(probs * grad_probs, axis=-1, keepdims=True)
        grad_scores = (probs * (grad_probs - inner)).astype(LOWTYPE)
        grad_query = jnp.einsum(
            "hgij,jhd->ihgd", grad_scores, keys, preferred_element_type=WIDETYPE
        ) * HD ** (-0.5)
        grad_keys = grad_keys + jnp.einsum(
            "hgij,ihgd->jhd", grad_scores, query_block, preferred_element_type=WIDETYPE
        ) * HD ** (-0.5)
        grad_values = grad_values + jnp.einsum(
            "hgij,ihgd->jhd", probs.astype(LOWTYPE), grad_block, preferred_element_type=WIDETYPE
        )
        return ((grad_keys, grad_values), grad_query)

    zeros_kv = jnp.zeros((seq_len, KV, HD), WIDETYPE)
    (grad_keys, grad_values), grad_queries = lax.scan(
        one_block, (zeros_kv, zeros_kv), (grouped, grad_grouped, logsum, starts)
    )
    return (grad_queries.reshape(seq_len, HQ, HD), grad_keys, grad_values)


def layer_forward(layer_input, length, weights):
    gain_one, w_query, w_key, w_value, w_out, gain_two, w_gate, w_up, w_down = weights
    seq_len = layer_input.shape[0]
    cosine_table, sine_table = tables(seq_len)
    normed_one = rms_scale(layer_input, gain_one.astype(WIDETYPE)).astype(LOWTYPE)
    query_pre = matmul(normed_one, w_query).reshape(seq_len, HQ, HD)
    key_pre = matmul(normed_one, w_key).reshape(seq_len, KV, HD)
    values = matmul(normed_one, w_value).astype(LOWTYPE).reshape(seq_len, KV, HD)
    queries = rotate(query_pre, cosine_table, sine_table).astype(LOWTYPE)
    keys = rotate(key_pre, cosine_table, sine_table).astype(LOWTYPE)
    mixed, logsum = attend_forward(queries.reshape(seq_len, KV, HQ // KV, HD), keys, values, length)
    resid = layer_input + matmul(mixed, w_out)
    normed_two = rms_scale(resid, gain_two.astype(WIDETYPE)).astype(LOWTYPE)
    gate = matmul(normed_two, w_gate)
    upper = matmul(normed_two, w_up)
    hidden = (jax.nn.silu(gate) * upper).astype(LOWTYPE)
    output = resid + matmul(hidden, w_down)
    return (
        output,
        (normed_one, queries, keys, values, logsum, mixed, resid, normed_two, gate, upper, hidden),
    )


def layer_backward(layer_input, length, weights, saved, grad_output):
    gain_one, w_query, w_key, w_value, w_out, gain_two, w_gate, w_up, w_down = weights
    normed_one, queries, keys, values, logsum, mixed, resid, normed_two, gate, upper, hidden = saved
    seq_len = layer_input.shape[0]
    cosine_table, sine_table = tables(seq_len)
    grad_low = grad_output.astype(LOWTYPE)
    grad_hidden = times_t(grad_low, w_down)
    silu_gate, silu_back = jax.vjp(jax.nn.silu, gate)
    grad_gate = silu_back(grad_hidden * upper)[0].astype(LOWTYPE)
    grad_up = (grad_hidden * silu_gate).astype(LOWTYPE)
    grad_normed_two = times_t(grad_gate, w_gate) + times_t(grad_up, w_up)
    _, norm_back_two = jax.vjp(rms_scale, resid, gain_two.astype(WIDETYPE))
    grad_resid_norm, grad_gain_two = norm_back_two(grad_normed_two)
    grad_resid = grad_output + grad_resid_norm
    grad_branch = grad_resid.astype(LOWTYPE)
    grad_mixed = times_t(grad_branch, w_out).astype(LOWTYPE)
    grad_query_rot, grad_key_rot, grad_value_sum = attend_backward(
        queries.reshape(seq_len, KV, HQ // KV, HD), keys, values, logsum, grad_mixed, length
    )
    _, rope_back = jax.vjp(
        lambda rotated: rotate(rotated, cosine_table, sine_table), grad_query_rot
    )
    grad_query = rope_back(grad_query_rot)[0].reshape(seq_len, HQ * HD).astype(LOWTYPE)
    _, rope_back_keys = jax.vjp(
        lambda rotated: rotate(rotated, cosine_table, sine_table), grad_key_rot
    )
    grad_key = rope_back_keys(grad_key_rot)[0].reshape(seq_len, KV * HD).astype(LOWTYPE)
    grad_value = grad_value_sum.reshape(seq_len, KV * HD).astype(LOWTYPE)
    grad_normed_one = (
        times_t(grad_query, w_query) + times_t(grad_key, w_key) + times_t(grad_value, w_value)
    )
    _, norm_back_one = jax.vjp(rms_scale, layer_input, gain_one.astype(WIDETYPE))
    grad_input_norm, grad_gain_one = norm_back_one(grad_normed_one)
    grad_input = grad_resid + grad_input_norm
    pieces = (
        grad_gain_one,
        normed_one,
        grad_query,
        grad_key,
        grad_value,
        mixed,
        grad_branch,
        grad_gain_two,
        normed_two,
        grad_gate,
        grad_up,
        hidden,
        grad_low,
    )
    return (grad_input, pieces)


def weight_grads(pieces):
    (
        grad_gain_one,
        normed_one,
        grad_query,
        grad_key,
        grad_value,
        mixed,
        grad_branch,
        grad_gain_two,
        normed_two,
        grad_gate,
        grad_up,
        hidden,
        grad_low,
    ) = pieces
    return (
        grad_gain_one,
        t_times(normed_one, grad_query),
        t_times(normed_one, grad_key),
        t_times(normed_one, grad_value),
        t_times(mixed, grad_branch),
        grad_gain_two,
        t_times(normed_two, grad_gate),
        t_times(normed_two, grad_up),
        t_times(hidden, grad_low),
    )


def stack_leaves(*leaves):
    return jnp.stack(leaves)


def local(
    boundary, lengths, gain_attn, w_query, w_key, w_value, w_out, gain_mlp, w_gate, w_up, w_down
):
    section = lax.axis_index("section")
    is_first = section == 0
    micro_count = boundary.shape[1]
    own_rows = boundary[0]
    seq_lengths = lengths[:, 0]
    gathered = turned_gather(
        (gain_attn, w_query, w_key, w_value, w_out, gain_mlp, w_gate, w_up, w_down),
        "dp",
        (1, 1, 1, 1, 2, 1, 1, 1, 2),
    )
    weights = tuple((whole[0] for whole in gathered))
    received = jnp.zeros(own_rows.shape[1:], LOWTYPE)
    layer_inputs = []
    layer_outputs = []
    kept_saved = []
    for position in range(micro_count + 1):
        current = min(position, micro_count - 1)
        entering = jnp.where(is_first, own_rows[current], received)
        index = jnp.clip(position - section, 0, micro_count - 1)
        length = lax.dynamic_index_in_dim(seq_lengths, index, keepdims=False)
        output, saved = layer_forward(entering.astype(WIDETYPE), length, weights)
        layer_inputs.append(entering)
        layer_outputs.append(output)
        kept_saved.append(saved)
        if position < micro_count:
            received = from_behind(output.astype(LOWTYPE), "section", 1)
    stacked_inputs = jnp.stack(layer_inputs)
    stacked_saved = jax.tree.map(stack_leaves, *kept_saved)
    regathered = turned_gather(
        (gain_attn, w_query, w_key, w_value, w_out, gain_mlp, w_gate, w_up, w_down),
        "dp",
        (1, 1, 1, 1, 2, 1, 1, 1, 2),
    )
    back_weights = tuple((whole[0] for whole in regathered))
    grad_received = jnp.zeros(own_rows.shape[1:], LOWTYPE)
    grads_in = []
    totals = None
    for position in range(micro_count + 1):
        batch = position + section - 1
        valid = (batch >= 0) & (batch < micro_count)
        index = jnp.clip(batch, 0, micro_count - 1)
        slot = jnp.clip(batch + section, 0, micro_count)
        length = lax.dynamic_index_in_dim(seq_lengths, index, keepdims=False)
        entering = lax.dynamic_index_in_dim(stacked_inputs, slot, keepdims=False).astype(WIDETYPE)
        saved = jax.tree.map(
            lambda stacked: lax.dynamic_index_in_dim(stacked, slot, keepdims=False), stacked_saved
        )
        current = min(position, micro_count - 1)
        grad_output = jnp.where(
            is_first, grad_received.astype(WIDETYPE), own_rows[current].astype(WIDETYPE)
        )
        grad_input, pieces = layer_backward(entering, length, back_weights, saved, grad_output)
        grads_in.append(grad_input)
        if position < micro_count:
            grad_received = from_behind(grad_input.astype(LOWTYPE), "section", -1)
        terms = tuple((jnp.where(valid, term, 0.0)[None] for term in weight_grads(pieces)))
        totals = (
            terms if totals is None else tuple((left + right for left, right in zip(totals, terms)))
        )
    totals = (
        lax.psum_scatter(totals[0], "dp", scatter_dimension=1, tiled=True),
        lax.psum_scatter(totals[1], "dp", scatter_dimension=1, tiled=True),
        lax.psum_scatter(totals[2], "dp", scatter_dimension=1, tiled=True),
        lax.psum_scatter(totals[3], "dp", scatter_dimension=1, tiled=True),
        lax.psum_scatter(totals[4], "dp", scatter_dimension=2, tiled=True),
        lax.psum_scatter(totals[5], "dp", scatter_dimension=1, tiled=True),
        lax.psum_scatter(totals[6], "dp", scatter_dimension=1, tiled=True),
        lax.psum_scatter(totals[7], "dp", scatter_dimension=1, tiled=True),
        lax.psum_scatter(totals[8], "dp", scatter_dimension=2, tiled=True),
    )
    ends = jnp.where(is_first, jnp.stack(grads_in[1:]), jnp.stack(layer_outputs[1:]))[None]
    return (
        ends,
        totals[0],
        totals[1],
        totals[2],
        totals[3],
        totals[4],
        totals[5],
        totals[6],
        totals[7],
        totals[8],
    )


def solution(mesh):
    in_specs = (
        P("section", None, "dp", None),
        P(None, "dp"),
        P("section", "dp"),
        P("section", "dp", None),
        P("section", "dp", None),
        P("section", "dp", None),
        P("section", None, "dp"),
        P("section", "dp"),
        P("section", "dp", None),
        P("section", "dp", None),
        P("section", None, "dp"),
    )
    out_specs = (
        P("section", None, "dp", None),
        P("section", "dp"),
        P("section", "dp", None),
        P("section", "dp", None),
        P("section", "dp", None),
        P("section", None, "dp"),
        P("section", "dp"),
        P("section", "dp", None),
        P("section", "dp", None),
        P("section", None, "dp"),
    )
    return jax.shard_map(local, mesh=mesh, in_specs=in_specs, out_specs=out_specs, check_vma=False)
```

profile of v0, /device:TPU:0, one launch (start us, length us, event | category | flops | bytes accessed | tf_op | source)
XLA Modules:
  0.0 1058.7 jit_solution(3429762565910577734)
XLA Ops:
  20.3 111.8 %all-gather.3.cloned.1.call-done = bf16[64,15,10242]{2,1,0:T(8,128)(2,1)} async-done(((bf16[1,15,10242]{2,1,0:T(8,128)(2,1)}), bf16[64,15,10242]{2,1,0:T(8,128)(2,1)}) %all-gather.3.cloned.1.call-update) | async-done | bytes 19664656 | tf_op jit(solution)/shard_map/all_gather | solution.py:22
  132.1 20.0 %reshape.955 = bf16[960,10242]{1,0:T(8,128)(2,1)} reshape(bf16[64,15,10242]{2,1,0:T(8,128)(2,1)} %all-gather.3.cloned.1.call-done) | data formatting | bytes 39329280
  155.1 2.5 slice_bitcast_fusion.24
  158.7 2.2 convolution_convert_fusion.8
  162.5 3.0 copy.70
  165.5 2.3 fusion.284
  168.9 2.6 multiply_reduce_fusion.5
  171.5 4.8 fusion.16
  176.3 6.5 multiply_convert_fusion.2
  182.8 5.4 fusion.94
  188.2 2.5 collective-permute-start
  192.9 2.4 convolution_convert_fusion.7
  195.3 2.3 fusion.181
  197.6 3.7 fusion.112
  202.2 2.8 multiply_reduce_fusion.4
  205.1 4.8 fusion.14
  209.9 5.1 multiply_convert_fusion.1
  215.2 3.1 fusion.357
  230.8 3.4 multiply_convert_fusion
  235.8 2.6 fusion.77
  240.5 2.8 fusion.166
  252.5 2.6 fusion.217
  255.2 2.6 fusion.228
  257.8 2.4 fusion.72
  263.1 2.7 fusion.162
  269.8 2.6 fusion.215
  273.6 2.6 fusion.224
  282.2 2.4 fusion.67
  287.5 2.8 fusion.158
  297.5 5.1 copy.85
  302.6 2.5 fusion.32
  305.1 4.8 copy.84
  309.9 4.9 add_bitcast_fusion.3
  314.8 11.0 %copy.86 = f32[1,960,960]{1,0,2:T(1,128)} copy(f32[1,960,960]{2,1,0:T(8,128)} %add_bitcast_fusion.3) | data formatting | bytes 7372800 | tf_op jit(solution)/shard_map/add | solution.py:312
  325.8 3.0 add_bitcast_fusion.4
  328.9 5.9 copy.83
  339.9 4.7 add_bitcast_fusion.1
  344.6 13.2 %copy.88 = f32[1,960,2560]{2,0,1:T(1,128)} copy(f32[1,960,2560]{2,1,0:T(8,128)} %add_bitcast_fusion.1) | data formatting | bytes 19660800 | tf_op jit(solution)/shard_map/add | solution.py:312
  361.8 5.1 add_bitcast_fusion.2
  366.9 13.3 %copy.87 = f32[1,960,2560]{2,0,1:T(1,128)} copy(f32[1,960,2560]{2,1,0:T(8,128)} %add_bitcast_fusion.2) | data formatting | bytes 19660800 | tf_op jit(solution)/shard_map/add | solution.py:312
  385.7 5.0 add_bitcast_fusion
  390.7 13.2 %copy.89 = f32[1,2560,960]{1,0,2:T(1,128)} copy(f32[1,2560,960]{1,2,0:T(8,128)} %add_bitcast_fusion) | data formatting | bytes 19660800 | tf_op jit(solution)/shard_map/add | solution.py:312
  405.8 5.3 fusion.93
  414.5 3.3 fusion.154
  417.8 180.9 %all-reduce.21 = (f32[1,960]{1,0:T(1,128)S(1)}, f32[1,960]{1,0:T(1,128)S(1)}) all-reduce(f32[1,960]{1,0:T(1,128)S(1)} %bitcast.776, f32[1,960]{1,0:T(1,128)S(1)} %bitcast.775), channel_id=2, replica_groups=mesh['section'=2,'dp'=64] {'dp'}, use_global_device_ids=true, to_apply=%region_30.31.clone | all-reduce | flops 1920 | bytes 15360
  608.9 87.0 %all-reduce.30.cloned.1.call-done = f32[1,960,2560]{2,0,1:T(1,128)} async-done(((f32[1,960,2560]{2,0,1:T(1,128)}), f32[1,960,2560]{2,0,1:T(1,128)}) %all-reduce.30.cloned.1.call-update) | async-done | bytes 9830416
  697.4 175.8 %all-reduce.28.cloned.1.call-done = f32[1,960,2560]{2,0,1:T(1,128)} async-done(((f32[1,960,2560]{2,0,1:T(1,128)}), f32[1,960,2560]{2,0,1:T(1,128)}) %all-reduce.28.cloned.1.call-update) | async-done | bytes 9830416
  874.8 175.6 %all-reduce.32.cloned.1.call-done = f32[1,2560,960]{1,0,2:T(1,128)} async-done(((f32[1,2560,960]{1,0,2:T(1,128)}), f32[1,2560,960]{1,0,2:T(1,128)}) %all-reduce.32.cloned.1.call-update) | async-done | bytes 9830416
  (364 shorter events, 105.6 us)
Async XLA Ops:
  7.2 124.9 %all-gather.3.cloned.1.call-start = ((), (), s32[]{:S(2)}) async-start(), calls=%async_computation | async-start | bytes 21565440 | tf_op jit(solution)/shard_map/all_gather | solution.py:22
  10.8 592.5 %all-reduce.34.cloned.1.call-start = ((), (), s32[]{:S(2)}) async-start(), calls=%async_computation.4 | async-start | bytes 21626880
  17.9 147.6 %copy-start.83 = (f32[128]{0:T(128)}, f32[128]{0:T(128)S(1)}, u32[]{:S(2)}) copy-start(f32[128]{0:T(128)S(1)} %add_rsqrt_fusion.5) | copy-start | bytes 1540
  152.1 6.6 copy-start
  153.5 124.2 %copy-start.55 = (f32[960]{0:T(1024)}, f32[960]{0:T(1024)S(1)}, u32[]{:S(2)}) copy-start(f32[960]{0:T(1024)S(1)} %get-tuple-element.164) | copy-start | bytes 11524
  153.5 136.8 %copy-start.43 = (f32[960]{0:T(1024)}, f32[960]{0:T(1024)S(1)}, u32[]{:S(2)}) copy-start(f32[960]{0:T(1024)S(1)} %get-tuple-element.153) | copy-start | bytes 11524
  160.9 7.6 copy-start.57
  162.5 5.5 copy-start.71
  168.9 7.4 copy-start.45
  171.5 11.3 %copy-start.7 = (f32[128,960]{0,1:T(8,128)}, f32[128,960]{0,1:T(8,128)S(1)}, u32[]{:S(2)}) copy-start(f32[128,960]{0,1:T(8,128)S(1)} %get-tuple-element.263) | copy-start | bytes 1474564
  171.5 11.3 %copy-start.77 = (f32[128]{0:T(128)}, f32[128]{0:T(128)S(1)}, u32[]{:S(2)}) copy-start(f32[128]{0:T(128)S(1)} %add_rsqrt_fusion.4) | copy-start | bytes 1540
  176.3 6.5 copy-start.5
  182.8 7.9 copy-start.85
  182.8 32.3 %slice-start = ((s8[19906560]{0:T(1024)(128)(4,1)}), s8[3129344]{0:T(1024)(128)(4,1)S(1)}, s32[]{:S(2)}) async-start(s8[19906560]{0:T(1024)(128)(4,1)} %bitcast.683), calls=%async_computation.5 | async-start | bytes 6258688
  188.2 3.6 collective-permute-start
  191.8 9.6 copy-start.70
  192.9 22.2 %slice-start.1 = ((s8[19906560]{0:T(1024)(128)(4,1)}), s8[4194304]{0:T(1024)(128)(4,1)S(1)}, s32[]{:S(2)}) async-start(s8[19906560]{0:T(1024)(128)(4,1)} %bitcast.683), calls=%async_computation.6 | async-start | bytes 8388608
  195.3 6.6 copy-start.59
  201.7 13.4 %slice-start.2 = ((s8[19906560]{0:T(1024)(128)(4,1)}), s8[4194304]{0:T(1024)(128)(4,1)S(1)}, s32[]{:S(2)}) async-start(s8[19906560]{0:T(1024)(128)(4,1)} %bitcast.683), calls=%async_computation.7 | async-start | bytes 8388608
  202.2 7.7 copy-start.47
  205.1 23.3 %copy-start.12 = (f32[128,960]{0,1:T(8,128)}, f32[128,960]{0,1:T(8,128)S(1)}, u32[]{:S(2)}) copy-start(f32[128,960]{0,1:T(8,128)S(1)} %get-tuple-element.269) | copy-start | bytes 1474564
  205.1 10.0 copy-start.79
  205.1 10.0 slice-start.3
  218.3 3.0 collective-permute-start.1
  243.5 34.3 %copy-start.16 = (bf16[3,128,960]{1,2,0:T(8,128)(2,1)}, bf16[3,128,960]{1,2,0:T(8,128)(2,1)S(1)}, u32[]{:S(2)}) copy-start(bf16[3,128,960]{1,2,0:T(8,128)(2,1)S(1)} %pad_maximum_fusion.4) | copy-start | bytes 2211844
  250.7 7.1 collective-permute-start.2
  252.5 17.3 %copy-start.18 = (bf16[3,128,960]{1,2,0:T(8,128)(2,1)}, bf16[3,128,960]{1,2,0:T(8,128)(2,1)S(1)}, u32[]{:S(2)}) copy-start(bf16[3,128,960]{1,2,0:T(8,128)(2,1)S(1)} %pad_maximum_fusion.6) | copy-start | bytes 2211844
  255.2 40.8 %copy-start.3 = (bf16[3,128,960]{1,2,0:T(8,128)(2,1)}, bf16[3,128,960]{1,2,0:T(8,128)(2,1)S(1)}, u32[]{:S(2)}) copy-start(bf16[3,128,960]{1,2,0:T(8,128)(2,1)S(1)} %pad_maximum_fusion.5) | copy-start | bytes 2211844
  260.2 5.6 copy-start.32
  278.8 3.4 collective-permute-start.3
  282.2 8.1 copy-start.21
  284.6 5.7 copy-start.40
  296.0 6.6 copy-start.4
  302.6 7.3 copy-start.15
  314.8 11.0 %copy-start.23 = (f32[128,15,32]{0,2,1:T(8,128)S(1)}, f32[128,15,32]{0,2,1:T(8,128)}, u32[]{:S(2)}) copy-start(f32[128,15,32]{0,2,1:T(8,128)} %get-tuple-element.222) | copy-start | bytes 737284
  314.8 11.0 %copy-start.24 = (f32[128,15,32]{0,2,1:T(8,128)S(1)}, f32[128,15,32]{0,2,1:T(8,128)}, u32[]{:S(2)}) copy-start(f32[128,15,32]{0,2,1:T(8,128)} %get-tuple-element.223) | copy-start | bytes 737284
  334.9 361.0 %all-reduce.30.cloned.1.call-start = ((), (), s32[]{:S(2)}) async-start(), calls=%async_computation.2 | async-start | bytes 19660800
  357.8 515.4 %all-reduce.28.cloned.1.call-start = ((), (), s32[]{:S(2)}) async-start(), calls=%async_computation.1 | async-start | bytes 19660800
  380.2 670.2 %all-reduce.32.cloned.1.call-start = ((), (), s32[]{:S(2)}) async-start(), calls=%async_computation.3 | async-start | bytes 19660800
  403.9 7.2 copy-start.72
  403.9 7.2 copy-start.74
  403.9 7.2 copy-start.76
  405.8 8.7 copy-start.17
  405.8 8.7 copy-start.56
  411.1 6.7 copy-start.73
  411.1 6.7 copy-start.75
  412.7 188.4 %copy-start.19 = (f32[1,1,128,960]{2,3,1,0:T(8,128)S(1)}, f32[1,1,128,960]{2,3,1,0:T(8,128)}, u32[]{:S(2)}) copy-start(f32[1,1,128,960]{2,3,1,0:T(8,128)} %get-tuple-element.217) | copy-start | bytes 1474564
  412.8 188.4 %copy-start.42 = (f32[128,960]{0,1:T(8,128)S(1)}, f32[128,960]{0,1:T(8,128)}, u32[]{:S(2)}) copy-start(f32[128,960]{0,1:T(8,128)} %get-tuple-element.273) | copy-start | bytes 1474564
  (54 other events, 138.1 us)
Sparse Core Ops, SparseCore 0:
  11.4 120.5 all-gather.2
  335.0 182.4 all-reduce.33
  522.8 172.9 all-reduce.29
  701.1 172.1 all-reduce.27
  878.4 171.9 all-reduce.31
where the time goes:
time: 1060 us
  waiting for transfers between devices  551 us (52%)
  blocking collectives  181 us (17%)
  matrix products  159 us (15%)
  local copies, waits for them, and re-layouts  120 us (11%)
  other arithmetic  23.2 us (2%)
  between operations  16.6 us (2%)
    unnamed x9, waiting for transfers between devices  438 us
    unnamed x1, blocking collectives  181 us
    all_gather x1, waiting for transfers between devices, turned_gather(): whole = lax.all_gather(both, axis, axis=0, tiled=True)  112 us
    add x7, local copies, waits for them, and re-layouts, local(): left + right  66.6 us
    dot_general x21, matrix products, matmul(): return jnp.dot(left, right, preferred_element_type=WIDETYPE)  65.2 us
    dot_general x21, matrix products, t_times(): lax.dot_general(left, right, (((0,), (0,)), ((), ())), preferred_element_...  47.8 us
    unnamed x197, local copies, waits for them, and re-layouts  39.1 us
    dot_general x21, matrix products, times_t(): lax.dot_general(left, right, (((1,), (1,)), ((), ())), preferred_element_...  39 us
  transfers between devices with their start and end apart: 9, of which 6 were waited for; matrix products, arithmetic and copies ran while one was open for 10% of the time, Pallas kernels for 0%

commit v1 on v0

v1 whole, which is shorter than its diff:
```python
import numpy as np

import jax
import jax.numpy as jnp
from jax import lax
from jax.experimental import pallas as pl
from jax.experimental.pallas import tpu as pltpu
from jax.sharding import PartitionSpec as P

D = 960
DP = 1024
HQ = 15
KV = 5
GROUP = HQ // KV
HD = 64
FF = 2560
SEQ = 128
MICRO = 2
ROWS = MICRO * SEQ
RING = 4
SHARD = 15
PADDED = 16
EPS = 1e-05
NEG = -1e30
BASE = 10000.0
BF = jnp.bfloat16
F32 = jnp.float32
MESH = pl.DeviceIdType.MESH

C_Q = 0
C_O = 1024
C_KV = 2048
C_G = 2688
C_U = 5248
C_D = 7808
C_ALL = 10368
CHUNK = 512
CHUNKS = FF // CHUNK

STRIDES = (16, 4, 1)
ORDERS = ((0, 1, 2), (1, 2, 0), (2, 0, 1))


def make_pieces():
    pieces = []
    for start, tiles in ((C_D, (7, 7, 6)), (C_G, (13, 13, 14)), (C_Q, (7, 7, 7))):
        at = start
        for part, count in enumerate(tiles):
            left = (count + 1) // 2 if part != 1 else count // 2
            pieces.append((at, at + 128 * left, at + 128 * count, ORDERS[part]))
            at += 128 * count
    return pieces


PIECES = make_pieces()


def position():
    me = lax.axis_index("dp")
    return me, (me // 16, (me // 4) % 4, me % 4)


def neighbour(me, coords, axis, step):
    here = coords[axis]
    return me + ((here + step) % RING - here) * STRIDES[axis]


def block(ref, order, phase, coords, at, first, last, later_full):
    index = [None, None, None]
    for place, axis in enumerate(order):
        if place == phase:
            index[axis] = at
        elif (place > phase) == later_full:
            index[axis] = slice(None)
        else:
            index[axis] = coords[axis]
    return ref.at[index[0], index[1], index[2], :, first:last]


def remote(src, dst, send, recv, device):
    return pltpu.make_async_remote_copy(
        src_ref=src,
        dst_ref=dst,
        send_sem=send,
        recv_sem=recv,
        device_id={"dp": device},
        device_id_type=MESH,
    )


class Gather:
    def __init__(self, number, whole, send, recv, me, coords):
        self.first, self.mid, self.last, self.order = PIECES[number]
        self.whole, self.send, self.recv = whole, send.at[number], recv.at[number]
        self.me, self.coords = me, coords
        self.copies = []
        self.pending = []

    def go(self, phase, slot, at, first, last, step):
        axis = self.order[phase]
        view = block(self.whole, self.order, phase, self.coords, at, first, last, False)
        index = phase * 4 + slot
        copy = remote(
            view,
            view,
            self.send.at[index],
            self.recv.at[index],
            neighbour(self.me, self.coords, axis, step),
        )
        copy.start()
        self.copies.append(copy)
        return copy

    def step(self, number):
        phase, second = divmod(number, 2)
        for copy in self.pending:
            copy.wait_recv()
        self.pending = []
        if phase == 3:
            return
        here = self.coords[self.order[phase]]
        if not second:
            right = self.go(phase, 0, here, self.first, self.last, 1)
            left = self.go(phase, 1, here, self.first, self.last, -1)
        else:
            right = self.go(phase, 2, (here + 3) % RING, self.first, self.mid, 1)
            left = self.go(phase, 3, (here + 1) % RING, self.mid, self.last, -1)
        self.pending = [right, left]

    def finish(self):
        for copy in self.copies:
            copy.wait_send()


class Scatter:
    def __init__(self, number, whole, lands, send, recv, result, me, coords):
        self.first, self.mid, self.last, self.order = PIECES[number]
        self.whole, self.lands = whole, lands
        self.send, self.recv = send.at[number], recv.at[number]
        self.result = result
        self.me, self.coords = me, coords
        self.copies = []
        self.now = {}

    def view(self, phase, at, side):
        first, last = (self.first, self.mid) if side == 0 else (self.mid, self.last)
        return block(self.whole, self.order, phase, self.coords, at, first, last, True)

    def go(self, phase, slot, at, side, step):
        copy = remote(
            self.view(phase, at, side),
            self.lands[phase][side].at[slot],
            self.send.at[phase * 6 + side * 3 + slot],
            self.recv.at[phase * 6 + side * 3 + slot],
            neighbour(self.me, self.coords, self.order[phase], step),
        )
        copy.start()
        self.copies.append(copy)
        self.now[side, slot] = copy

    def add(self, phase, at, side, slots):
        view = self.view(phase, at, side)
        land = self.lands[phase][side]
        if phase == 2:
            total = view[...].astype(F32)
            for slot in slots:
                total = total + land[slot].astype(F32)
            if len(slots) == 2:
                first, last = (self.first, self.mid) if side == 0 else (self.mid, self.last)
                self.result[:, first:last] = total
            else:
                view[...] = total.astype(BF)
            return

        def one(step, carry):
            total = view[step].astype(F32)
            for slot in slots:
                total = total + land[slot, step].astype(F32)
            view[step] = total.astype(BF)
            return carry

        lax.fori_loop(0, RING, one, 0)

    def step(self, number):
        phase, part = divmod(number, 3)
        if phase == 3:
            return
        here = self.coords[self.order[phase]]
        ahead, across, behind = (here + 1) % RING, (here + 2) % RING, (here + 3) % RING
        if part == 0:
            self.go(phase, 0, across, 0, 1)
            self.go(phase, 0, across, 1, -1)
            self.go(phase, 1, ahead, 1, 1)
            self.go(phase, 1, behind, 0, -1)
        elif part == 1:
            self.now[0, 0].wait_recv()
            self.add(phase, ahead, 0, (0,))
            self.go(phase, 2, ahead, 0, 1)
            self.now[1, 0].wait_recv()
            self.add(phase, behind, 1, (0,))
            self.go(phase, 2, behind, 1, -1)
        else:
            for side in (0, 1):
                self.now[side, 1].wait_recv()
                self.now[side, 2].wait_recv()
                self.add(phase, here, side, (1, 2))

    def finish(self):
        for copy in self.copies:
            copy.wait_send()


def dot(left, right):
    return jnp.dot(left, right, preferred_element_type=F32)


def dot_nt(left, right):
    return lax.dot_general(left, right, (((1,), (1,)), ((), ())), preferred_element_type=F32)


def dot_tn(left, right):
    return lax.dot_general(left, right, (((0,), (0,)), ((), ())), preferred_element_type=F32)


def columns(whole, first, count):
    return whole[:, :, :, :, pl.ds(first, count)].reshape(DP, count)


def swap_halves(tile):
    lane = lax.broadcasted_iota(jnp.int32, tile.shape, 1)
    return jnp.where(lane % HD < HD // 2, pltpu.roll(tile, 96, 1), pltpu.roll(tile, 32, 1))


def norm_forward(matrix, gain):
    scale = lax.rsqrt(jnp.sum(matrix * matrix, axis=1, keepdims=True) * (1.0 / D) + EPS)
    return (matrix * scale * gain).astype(BF)


def norm_backward(matrix, gain, grad):
    scale = lax.rsqrt(jnp.sum(matrix * matrix, axis=1, keepdims=True) * (1.0 / D) + EPS)
    scaled = grad * gain
    inner = jnp.sum(scaled * matrix, axis=1, keepdims=True) * (1.0 / D)
    grad_matrix = scale * (scaled - matrix * (scale * scale * inner))
    grad_gain = jnp.sum(grad * matrix * scale, axis=0, keepdims=True)
    return grad_matrix, grad_gain


def kernel(
    shard,
    rows_in,
    lengths,
    cosine,
    sine,
    ends,
    result,
    whole,
    entering,
    grad_out,
    crossing,
    spread,
    normed_one,
    queries,
    key_value,
    probs,
    mixed,
    resid,
    normed_two,
    gate_up,
    hidden,
    total,
    grad_resid,
    grad_branch,
    grad_mixed,
    grad_kv,
    gains,
    grad_gains,
    gather_send,
    gather_recv,
    scatter_send,
    scatter_recv,
    cross_send,
    cross_recv,
    *lands,
):
    section = lax.axis_index("section")
    me, coords = position()
    is_first = section == 0

    barrier = pltpu.get_barrier_semaphore()
    for axis in range(3):
        for step in (1, -1):
            pl.semaphore_signal(
                barrier,
                inc=1,
                device_id={"dp": neighbour(me, coords, axis, step)},
                device_id_type=MESH,
            )
    pl.semaphore_signal(barrier, inc=1, device_id={"section": 1 - section}, device_id_type=MESH)
    whole[coords[0], coords[1], coords[2]] = shard[...]
    pl.semaphore_wait(barrier, 7)

    gathers = [
        Gather(number, whole, gather_send, gather_recv, me, coords)
        for number in range(len(PIECES))
    ]
    order = (6, 7, 8, 3, 4, 5, 0, 1, 2)
    for number in order:
        gathers[number].step(0)

    row = lax.broadcasted_iota(jnp.int32, (D, DP), 0)
    column = lax.broadcasted_iota(jnp.int32, (D, DP), 1)
    chosen = (column - column // PADDED == row) & (column % PADDED != SHARD)
    spread[...] = jnp.where(chosen, 1.0, 0.0).astype(BF)
    own_rows = dot(rows_in[...], spread[...]).astype(BF)

    @pl.when(is_first)
    def _():
        entering[...] = own_rows

    @pl.when(jnp.logical_not(is_first))
    def _():
        grad_out[...] = own_rows

    for tick in range(1, 9):
        for place in range(3):
            stage = tick - place
            if 1 <= stage <= 6:
                for number in order[3 * place : 3 * place + 3]:
                    gathers[number].step(stage)
    for number in order:
        gathers[number].finish()

    def cross(target, slot):
        return pltpu.make_async_remote_copy(
            src_ref=crossing,
            dst_ref=target,
            send_sem=cross_send.at[slot],
            recv_sem=cross_recv.at[slot],
            device_id={"section": 1 - section},
            device_id_type=MESH,
        )

    middle_copy = cross(entering, 0)
    grad_copy = cross(grad_out, 1)

    @pl.when(jnp.logical_not(is_first))
    def _():
        middle_copy.wait_recv()

    picks = jnp.where(
        lax.broadcasted_iota(jnp.int32, (PADDED, DP), 1) % PADDED == SHARD, 1.0, 0.0
    ).astype(BF)
    gains[0:1, :] = dot(picks, columns(whole, C_Q, DP))[0:1]
    gains[1:2, :] = dot(picks, columns(whole, C_G, DP))[0:1]
    matrix = entering[...].astype(F32)
    normed_one[...] = norm_forward(matrix, gains[0:1, :])

    cos_rows = jnp.concatenate([cosine[...]] * MICRO, axis=0)
    sin_rows = jnp.concatenate([sine[...]] * MICRO, axis=0)
    low_lane = lax.broadcasted_iota(jnp.int32, (ROWS, 128), 1) < HD

    for half in range(2):
        pre = dot(normed_one[...], columns(whole, C_Q + half * 512, 512))
        for tile in range(4):
            part = pre[:, tile * 128 : tile * 128 + 128]
            at = half * 512 + tile * 128
            queries[:, at : at + 128] = (part * cos_rows + swap_halves(part) * sin_rows).astype(BF)
    pre = dot(normed_one[...], columns(whole, C_KV, 640))
    for tile in range(5):
        part = pre[:, tile * 128 : tile * 128 + 128]
        if tile < 3:
            turned = part * cos_rows + swap_halves(part) * sin_rows
            part = turned if tile < 2 else jnp.where(low_lane, turned, part)
        key_value[:, tile * 128 : tile * 128 + 128] = part.astype(BF)

    def attend(seq, carry):
        rows = pl.ds(pl.multiple_of(seq * SEQ, SEQ), SEQ)
        query_pos = lax.broadcasted_iota(jnp.int32, (GROUP, SEQ, SEQ), 1).reshape(GROUP * SEQ, SEQ)
        key_pos = lax.broadcasted_iota(jnp.int32, (GROUP * SEQ, SEQ), 1)
        allowed = (key_pos <= query_pos) & (key_pos < lengths[seq, 0])
        query_rows = queries[rows, :]
        kv_rows = key_value[rows, :]
        heads = []
        for group in range(KV):
            at = group * GROUP * HD
            query = jnp.concatenate(
                [query_rows[:, at + h * HD : at + h * HD + HD] for h in range(GROUP)], axis=0
            )
            key = kv_rows[:, group * HD : group * HD + HD]
            value = kv_rows[:, (KV + group) * HD : (KV + group) * HD + HD]
            scores = jnp.where(allowed, dot_nt(query, key) * HD**-0.5, NEG)
            expos = jnp.exp(scores - jnp.max(scores, axis=1, keepdims=True))
            chances = expos / jnp.sum(expos, axis=1, keepdims=True)
            probs[seq, group] = chances
            out = dot(chances.astype(BF), value)
            heads.extend(out[h * SEQ : h * SEQ + SEQ] for h in range(GROUP))
        heads.append(jnp.zeros((SEQ, HD), F32))
        mixed[rows, :] = jnp.concatenate(heads, axis=1).astype(BF)
        return carry

    lax.fori_loop(0, MICRO, attend, 0)
    matrix = entering[...].astype(F32) + dot_nt(mixed[...], columns(whole, C_O, DP))
    resid[...] = matrix
    normed_two[...] = norm_forward(matrix, gains[1:2, :])
    total[...] = matrix

    def feed(step, carry):
        at = pl.multiple_of(step * CHUNK, CHUNK)
        here = pl.ds(at, CHUNK)
        gates = dot(normed_two[...], columns(whole, C_G + at, CHUNK))
        uppers = dot(normed_two[...], columns(whole, C_U + at, CHUNK))
        gate_up[:, here] = gates.astype(BF)
        gate_up[:, pl.ds(FF + at, CHUNK)] = uppers.astype(BF)
        hiddens = (gates / (1.0 + jnp.exp(-gates)) * uppers).astype(BF)
        hidden[:, here] = hiddens
        total[...] += dot_nt(hiddens, columns(whole, C_D + at, CHUNK))
        return carry

    lax.fori_loop(0, CHUNKS, feed, 0)

    def narrow(value):
        high = value.astype(BF)
        low = (value - high.astype(F32)).astype(BF)
        return dot_nt(high, spread[...]) + dot_nt(low, spread[...])

    @pl.when(is_first)
    def _():
        crossing[...] = total[...].astype(BF)
        middle_copy.start()
        middle_copy.wait_send()
        grad_copy.wait_recv()

    @pl.when(jnp.logical_not(is_first))
    def _():
        ends[...] = narrow(total[...])

    total[...] = jnp.zeros_like(total)

    def feed_back(step, carry):
        at = pl.multiple_of(step * CHUNK, CHUNK)
        here, beyond = pl.ds(at, CHUNK), pl.ds(FF + at, CHUNK)
        grad_hidden = dot(grad_out[...], columns(whole, C_D + at, CHUNK))
        gates = gate_up[:, here].astype(F32)
        opened = 1.0 / (1.0 + jnp.exp(-gates))
        grad_gate = (
            grad_hidden * gate_up[:, beyond].astype(F32) * (opened * (1.0 + gates * (1.0 - opened)))
        ).astype(BF)
        grad_up = (grad_hidden * (gates * opened)).astype(BF)
        gate_up[:, here] = grad_gate
        gate_up[:, beyond] = grad_up
        total[...] += dot_nt(grad_gate, columns(whole, C_G + at, CHUNK)) + dot_nt(
            grad_up, columns(whole, C_U + at, CHUNK)
        )
        return carry

    lax.fori_loop(0, CHUNKS, feed_back, 0)
    through, grad_gain = norm_backward(resid[...], gains[1:2, :], total[...])
    grad_gains[...] = jnp.zeros_like(grad_gains)
    grad_gains[1:2, 0:DP] = grad_gain
    through = through + grad_out[...].astype(F32)
    grad_resid[...] = through
    grad_branch[...] = through.astype(BF)
    grad_mixed[...] = dot(grad_branch[...], columns(whole, C_O, DP)).astype(BF)

    def attend_back(seq, carry):
        rows = pl.ds(pl.multiple_of(seq * SEQ, SEQ), SEQ)
        query_rows = queries[rows, :]
        kv_rows = key_value[rows, :]
        grad_rows = grad_mixed[rows, :]
        query_parts = []
        key_parts = []
        value_parts = []
        for group in range(KV):
            at = group * GROUP * HD
            query = jnp.concatenate(
                [query_rows[:, at + h * HD : at + h * HD + HD] for h in range(GROUP)], axis=0
            )
            grad = jnp.concatenate(
                [grad_rows[:, at + h * HD : at + h * HD + HD] for h in range(GROUP)], axis=0
            )
            key = kv_rows[:, group * HD : group * HD + HD]
            value = kv_rows[:, (KV + group) * HD : (KV + group) * HD + HD]
            chances = probs[seq, group]
            grad_probs = dot_nt(grad, value)
            inner = jnp.sum(chances * grad_probs, axis=1, keepdims=True)
            grad_scores = (chances * (grad_probs - inner)).astype(BF)
            grad_query = dot(grad_scores, key) * HD**-0.5
            query_parts.extend(grad_query[h * SEQ : h * SEQ + SEQ] for h in range(GROUP))
            key_parts.append(dot_tn(grad_scores, query) * HD**-0.5)
            value_parts.append(dot_tn(chances.astype(BF), grad))
        query_parts.append(jnp.zeros((SEQ, HD), F32))
        total[rows, :] = jnp.concatenate(query_parts, axis=1)
        grad_kv[rows, :] = jnp.concatenate(key_parts + value_parts, axis=1)
        return carry

    lax.fori_loop(0, MICRO, attend_back, 0)
    grad_query = grad_mixed
    for tile in range(8):
        part = total[:, tile * 128 : tile * 128 + 128]
        grad_query[:, tile * 128 : tile * 128 + 128] = (
            part * cos_rows - swap_halves(part) * sin_rows
        ).astype(BF)
    for tile in range(5):
        part = grad_kv[:, tile * 128 : tile * 128 + 128]
        if tile < 3:
            turned = part * cos_rows - swap_halves(part) * sin_rows
            part = turned if tile < 2 else jnp.where(low_lane, turned, part)
        key_value[:, tile * 128 : tile * 128 + 128] = part.astype(BF)
    grad_normed = dot_nt(grad_query[...], columns(whole, C_Q, DP)) + dot_nt(
        key_value[...], columns(whole, C_KV, 640)
    )
    through, grad_gain = norm_backward(entering[...].astype(F32), gains[0:1, :], grad_normed)
    grad_gains[0:1, 0:DP] = grad_gain
    through = through + grad_resid[...]

    @pl.when(is_first)
    def _():
        ends[...] = narrow(through)

    @pl.when(jnp.logical_not(is_first))
    def _():
        crossing[...] = through.astype(BF)
        grad_copy.start()
        grad_copy.wait_send()

    def put(left, right, first, count, gain):
        grad = dot_tn(left, right)
        if gain is not None:
            at, gain_row = gain
            row = lax.broadcasted_iota(jnp.int32, (DP, count), 0)
            column = lax.broadcasted_iota(jnp.int32, (DP, count), 1) + at
            own = (row % PADDED == SHARD) & (row // PADDED == column // PADDED)
            grad = jnp.where(own, gain_row, grad)
        whole[:, :, :, :, pl.ds(first, count)] = grad.astype(BF).reshape(4, 4, 4, PADDED, count)

    number_of = len(PIECES)
    scatters = [
        Scatter(
            number,
            whole,
            [lands[6 * number + 2 * phase : 6 * number + 2 * phase + 2] for phase in range(3)],
            scatter_send,
            scatter_recv,
            result,
            me,
            coords,
        )
        for number in range(number_of)
    ]

    def put_down(step, carry):
        at = pl.multiple_of(step * CHUNK, CHUNK)
        put(grad_out[...], hidden[:, pl.ds(at, CHUNK)], C_D + at, CHUNK, None)
        return carry

    lax.fori_loop(0, CHUNKS, put_down, 0)
    for number in (0, 1, 2):
        scatters[number].step(0)

    def put_gate_up(step, carry):
        at = pl.multiple_of(step * CHUNK, CHUNK)
        gain = (at, grad_gains[1:2, pl.ds(at, CHUNK)])
        put(normed_two[...], gate_up[:, pl.ds(at, CHUNK)], C_G + at, CHUNK, gain)
        return carry

    lax.fori_loop(0, 2 * CHUNKS, put_gate_up, 0)
    for number in (3, 4, 5):
        scatters[number].step(0)
    for half in range(2):
        at = half * CHUNK
        gain = (at, grad_gains[0:1, at : at + CHUNK])
        put(normed_one[...], grad_query[:, at : at + CHUNK], C_Q + at, CHUNK, gain)
        put(grad_branch[...], mixed[:, at : at + CHUNK], C_O + at, CHUNK, None)
    put(normed_one[...], key_value[...], C_KV, 640, None)
    for number in (6, 7, 8):
        scatters[number].step(0)

    for tick in range(1, 11):
        for place in range(3):
            stage = tick - place
            if 1 <= stage <= 8:
                for number in range(3 * place, 3 * place + 3):
                    scatters[number].step(stage)
    for number in range(number_of):
        scatters[number].finish()


def rope_tables():
    frequency = BASE ** (-(np.arange(HD // 2, dtype=np.float32) * np.float32(2.0 / HD)))
    angles = np.arange(SEQ, dtype=np.float32)[:, None] * frequency[None, :].astype(np.float32)
    cos, sin = np.cos(angles), np.sin(angles)
    return (
        np.concatenate([cos, cos, cos, cos], axis=1).astype(np.float32),
        np.concatenate([-sin, sin, -sin, sin], axis=1).astype(np.float32),
    )


def run_kernel(shard, rows_in, lengths, cosine, sine):
    scratch = [
        ((RING, RING, RING, PADDED, C_ALL), BF),
        ((ROWS, DP), BF),
        ((ROWS, DP), BF),
        ((ROWS, DP), BF),
        ((D, DP), BF),
        ((ROWS, DP), BF),
        ((ROWS, DP), BF),
        ((ROWS, 640), BF),
        ((MICRO, KV, GROUP * SEQ, SEQ), F32),
        ((ROWS, DP), BF),
        ((ROWS, DP), F32),
        ((ROWS, DP), BF),
        ((ROWS, 2 * FF), BF),
        ((ROWS, FF), BF),
        ((ROWS, DP), F32),
        ((ROWS, DP), F32),
        ((ROWS, DP), BF),
        ((ROWS, DP), BF),
        ((ROWS, 640), F32),
        ((8, DP), F32),
        ((8, 2 * FF), F32),
    ]
    scratch = [pltpu.VMEM(shape, kind) for shape, kind in scratch]
    count = len(PIECES)
    scratch += [
        pltpu.SemaphoreType.DMA((count, 12)),
        pltpu.SemaphoreType.DMA((count, 12)),
        pltpu.SemaphoreType.DMA((count, 18)),
        pltpu.SemaphoreType.DMA((count, 18)),
        pltpu.SemaphoreType.DMA((2,)),
        pltpu.SemaphoreType.DMA((2,)),
    ]
    for first, mid, last, _ in PIECES:
        for phase in range(3):
            for width in (mid - first, last - mid):
                shape = (3,) + (RING,) * (2 - phase) + (PADDED, width)
                scratch.append(pltpu.VMEM(shape, BF))
    vmem = pl.BlockSpec(memory_space=pltpu.VMEM)
    return pl.pallas_call(
        kernel,
        out_shape=(
            jax.ShapeDtypeStruct((ROWS, D), F32),
            jax.ShapeDtypeStruct((PADDED, C_ALL), F32),
        ),
        in_specs=[vmem, vmem, pl.BlockSpec(memory_space=pltpu.SMEM), vmem, vmem],
        out_specs=(vmem, vmem),
        scratch_shapes=scratch,
        compiler_params=pltpu.CompilerParams(
            collective_id=0, has_side_effects=True, vmem_limit_bytes=64 * 1024 * 1024
        ),
    )(shard, rows_in, lengths, cosine, sine)


def local(
    boundary, lengths, gain_attn, w_query, w_key, w_value, w_out, gain_mlp, w_gate, w_up, w_down
):
    me = lax.axis_index("dp")

    def pad(matrix, width):
        return jnp.pad(matrix, ((0, 0), (0, width - matrix.shape[1])))

    body = jnp.concatenate(
        [
            pad(w_query[0], 1024),
            pad(w_out[0].T, 1024),
            w_key[0],
            w_value[0],
            w_gate[0],
            w_up[0],
            w_down[0].T,
        ],
        axis=1,
    )
    ours = jnp.arange(DP // PADDED)[:, None] == me
    spread_one = jnp.where(ours, pad(gain_attn, PADDED), 0).reshape(1, DP)
    spread_two = jnp.where(ours, pad(gain_mlp, PADDED), 0).reshape(1, DP)
    last = jnp.concatenate(
        [
            spread_one,
            jnp.zeros((1, C_G - DP), BF),
            spread_two,
            jnp.zeros((1, C_ALL - C_G - DP), BF),
        ],
        axis=1,
    )
    shard = jnp.concatenate([body, last.astype(BF)], axis=0)
    cosine, sine = rope_tables()
    ends, result = run_kernel(
        shard,
        boundary[0].reshape(ROWS, D),
        lengths,
        jnp.asarray(cosine),
        jnp.asarray(sine),
    )
    body = result[:SHARD]

    def gain_of(first):
        return result[SHARD, first : first + DP].reshape(DP // PADDED, PADDED).sum(axis=0)[:SHARD]

    return (
        ends.reshape(1, MICRO, SEQ, D),
        gain_of(C_Q)[None],
        body[None, :, C_Q : C_Q + D],
        body[None, :, C_KV : C_KV + 320],
        body[None, :, C_KV + 320 : C_KV + 640],
        body[:, C_O : C_O + D].T[None],
        gain_of(C_G)[None],
        body[None, :, C_G : C_G + FF],
        body[None, :, C_U : C_U + FF],
        body[:, C_D : C_D + FF].T[None],
    )


def solution(mesh):
    row = P("section", "dp", None)
    column = P("section", None, "dp")
    gain = P("section", "dp")
    ends = P("section", None, "dp", None)
    weights = (gain, row, row, row, column, gain, row, row, column)
    return jax.shard_map(
        local,
        mesh=mesh,
        in_specs=(ends, P(None, "dp")) + weights,
        out_specs=(ends,) + weights,
        check_vma=False,
    )
```

time: 1060 us -> 253 us (0.24)
  waiting for transfers between devices: 551 us -> 0 us
  Pallas kernels: 0 us -> 234 us
  blocking collectives: 181 us -> 0 us
  matrix products: 159 us -> 0 us
  local copies, waits for them, and re-layouts: 120 us -> 16.4 us
  other arithmetic: 23.2 us -> 0.97 us
  between operations: 16.6 us -> 0.73 us
    unnamed x9 -> x0, waiting for transfers between devices: 438 us -> none
    pallas_call x0 -> x1, Pallas kernels: none -> 234 us  [run_kernel(): pl.pallas_call(kernel, out_shape=(jax.ShapeDtypeStruct((ROWS, D), F32), j...]
    unnamed x1 -> x0, blocking collectives: 181 us -> none
    dot_general x84 -> x0, matrix products: 159 us -> none  [the longest x21 65.2 us: matmul(): return jnp.dot(left, right, preferred_element_type=WIDETYPE)]
    all_gather x1 -> x0, waiting for transfers between devices: 112 us -> none  [turned_gather(): whole = lax.all_gather(both, axis, axis=0, tiled=True)]
    add x7 -> x0, local copies, waits for them, and re-layouts: 66.6 us -> none  [local(): left + right]
    unnamed x197 -> x24, local copies, waits for them, and re-layouts: 39.1 us -> 9.68 us
  transfers between devices with their start and end apart: 9 -> 0, of which waited for: 6 -> 0; matrix products, arithmetic and copies ran while one was open for 10% -> 0% of each run, Pallas kernels for 0% -> 0%
where the time goes in v1:
time: 253 us; the launch traced here: 252 us
  Pallas kernels  234 us (92%)
  local copies, waits for them, and re-layouts  16.4 us (6%)
    pallas_call x1, Pallas kernels, run_kernel(): pl.pallas_call(kernel, out_shape=(jax.ShapeDtypeStruct((ROWS, D), F32), j...  234 us
    unnamed x24, local copies, waits for them, and re-layouts  9.68 us

profile of v1, /device:TPU:0, one launch (start us, length us, event | category | flops | bytes accessed | tf_op | source)
XLA Modules:
  0.0 252.3 jit_solution(10266037556898796333)
XLA Ops:
  0.6 0.7 pad_bitcast_fusion
  1.3 0.0 copy-start.5
  1.3 0.0 copy-start.4
  1.3 0.1 broadcast_select_fusion.1
  1.4 0.1 select_n.28
  1.5 0.0 copy-start.2
  1.5 0.0 copy-start.3
  1.5 0.1 select_n.30
  1.6 0.5 copy-done.4
  2.1 0.0 copy-done.5
  2.1 0.3 copy-done.2
  2.4 0.0 copy-done.3
  2.5 1.0 concatenate.9
  3.5 0.0 copy-start.1
  3.5 0.8 maximum_maximum_fusion.shard
  4.3 0.2 copy-done.1
  4.5 1.0 copy.33
  5.5 0.0 copy-start.6
  5.5 0.7 copy-done.6
  6.2 0.6 copy.34.lengths
  6.8 234.2 %shard_map.204 = (f32[256,960]{1,0:T(8,128)}, f32[16,10368]{1,0:T(8,128)}) custom-call(bf16[16,10368]{1,0:T(8,128)(2,1)} %maximum_maximum_fusion.shard, bf16[256,960]{1,0:T(8,128)(2,1)} %bitcast.39, s32[2,1]{1,0:T(2,128)} %copy.34.lengths, f32[128,128]{1,0:T(8,128)} %constant.4.clone.cosine, f32[128,128]{1,0:T(8,128)} %constant.16.clone.sine), custom_call_target="tpu_custom_call" | custom-call | tf_op jit(solution)/shard_map/pallas_call | solution.py:638
  241.0 1.1 slice_bitcast_fusion
  242.1 0.0 copy-start
  242.1 0.8 copy.40
  242.9 0.8 copy.41
  243.7 0.8 copy.42
  244.6 0.9 slice_bitcast_fusion.3
  245.4 0.7 copy.36
  246.1 0.7 copy.39
  246.8 0.9 slice_bitcast_fusion.5
  247.7 0.6 copy.37
  248.3 0.6 copy.38
  249.0 0.8 slice_reduce_fusion
  249.8 0.1 reshape_squeeze.11
  249.9 0.5 slice_bitcast_fusion.7
  250.4 0.1 reshape_squeeze.10
  250.5 0.5 slice_bitcast_fusion.8
  251.0 0.0 copy-done
  251.0 1.3 copy.35
  (7 shorter events, 0.1 us)
Async XLA Ops:
  1.3 0.8 copy-start.5
  1.3 0.8 copy-start.4
  1.5 0.9 copy-start.2
  1.5 0.9 copy-start.3
  3.5 1.0 copy-start.1
  5.5 0.7 copy-start.6
  242.1 8.9 %copy-start = (f32[256,960]{1,0:T(8,128)S(1)}, f32[256,960]{1,0:T(8,128)}, u32[]{:S(2)}) copy-start(f32[256,960]{1,0:T(8,128)} %get-tuple-element.12) | copy-start | bytes 2949124

commit v2 on v1

--- a/solution.py
+++ b/solution.py
@@ -30,12 +30,11 @@
 C_Q = 0
 C_O = 1024
 C_KV = 2048
-C_G = 2688
-C_U = 5248
-C_D = 7808
-C_ALL = 10368
-CHUNK = 512
-CHUNKS = FF // CHUNK
+C_FF = 2688
+CHUNKS = (1024, 1024, 512)
+STARTS = (0, 1024, 2048)
+SUB = 512
+C_ALL = C_FF + 3 * FF
 
 STRIDES = (16, 4, 1)
 ORDERS = ((0, 1, 2), (1, 2, 0), (2, 0, 1))
@@ -43,16 +42,19 @@
 
 def make_pieces():
     pieces = []
-    for start, tiles in ((C_D, (7, 7, 6)), (C_G, (13, 13, 14)), (C_Q, (7, 7, 7))):
-        at = start
-        for part, count in enumerate(tiles):
-            left = (count + 1) // 2 if part != 1 else count // 2
-            pieces.append((at, at + 128 * left, at + 128 * count, ORDERS[part]))
-            at += 128 * count
+    for part in range(3):
+        at = 896 * part
+        pieces.append((at, at + (512 if part != 1 else 384), at + 896, ORDERS[part], at))
+    at = C_FF
+    for chunk, start in zip(CHUNKS, STARTS):
+        for part in range(3):
+            pieces.append((at, at + chunk // 2, at + chunk, ORDERS[part], C_FF + FF * part + start))
+            at += chunk
     return pieces
 
 
 PIECES = make_pieces()
+GROUPS = len(CHUNKS) + 1
 
 
 def position():
@@ -90,7 +92,7 @@
 
 class Gather:
     def __init__(self, number, whole, send, recv, me, coords):
-        self.first, self.mid, self.last, self.order = PIECES[number]
+        self.first, self.mid, self.last, self.order, _ = PIECES[number]
         self.whole, self.send, self.recv = whole, send.at[number], recv.at[number]
         self.me, self.coords = me, coords
         self.copies = []
@@ -134,7 +136,7 @@
 
 class Scatter:
     def __init__(self, number, whole, lands, send, recv, result, me, coords):
-        self.first, self.mid, self.last, self.order = PIECES[number]
+        self.first, self.mid, self.last, self.order, self.home = PIECES[number]
         self.whole, self.lands = whole, lands
         self.send, self.recv = send.at[number], recv.at[number]
         self.result = result
@@ -166,8 +168,9 @@
             for slot in slots:
                 total = total + land[slot].astype(F32)
             if len(slots) == 2:
-                first, last = (self.first, self.mid) if side == 0 else (self.mid, self.last)
-                self.result[:, first:last] = total
+                first = self.home if side == 0 else self.home + self.mid - self.first
+                for row in range(PADDED):
+                    self.result[row, :, first : first + total.shape[1]] = total[row : row + 1]
             else:
                 view[...] = total.astype(BF)
             return
@@ -246,13 +249,22 @@
 
 
 def kernel(
-    shard,
+    w_query,
+    w_out,
+    w_key,
+    w_value,
+    w_gate,
+    w_up,
+    w_down,
+    gain_attn,
+    gain_mlp,
     rows_in,
     lengths,
     cosine,
     sine,
     ends,
     result,
+    gain_result,
     whole,
     entering,
     grad_out,
@@ -268,6 +280,7 @@
     gate_up,
     hidden,
     total,
+    total_back,
     grad_resid,
     grad_branch,
     grad_mixed,
@@ -280,6 +293,7 @@
     scatter_recv,
     cross_send,
     cross_recv,
+    turn,
     *lands,
 ):
     section = lax.axis_index("section")
@@ -296,22 +310,59 @@
                 device_id_type=MESH,
             )
     pl.semaphore_signal(barrier, inc=1, device_id={"section": 1 - section}, device_id_type=MESH)
-    whole[coords[0], coords[1], coords[2]] = shard[...]
+
+    unit = jnp.where(
+        lax.broadcasted_iota(jnp.int32, (PADDED, SHARD), 0)
+        == lax.broadcasted_iota(jnp.int32, (PADDED, SHARD), 1),
+        1.0,
+        0.0,
+    ).astype(BF)
+    place = jnp.where(
+        lax.broadcasted_iota(jnp.int32, (SHARD, DP), 1)
+        == lax.broadcasted_iota(jnp.int32, (SHARD, DP), 0) + me * PADDED,
+        1.0,
+        0.0,
+    ).astype(BF)
+    last_row = lax.broadcasted_iota(jnp.int32, (PADDED, DP), 0) == SHARD
+
+    def set_block(first, value):
+        whole[coords[0], coords[1], coords[2], :, first : first + value.shape[1]] = value.astype(BF)
+
+    def with_gain(weights, gain):
+        body = jnp.concatenate(
+            [dot(unit, weights[...]), jnp.zeros((PADDED, DP - D), F32)], axis=1
+        )
+        return jnp.where(last_row, dot(gain[...], place), body)
+
+    set_block(C_Q, with_gain(w_query, gain_attn))
+    set_block(C_O, with_gain(w_out, gain_mlp))
+    set_block(C_KV, jnp.concatenate([dot(unit, w_key[...]), dot(unit, w_value[...])], axis=1))
+    for index, (chunk, start) in enumerate(zip(CHUNKS, STARTS)):
+        for part, weights in enumerate((w_gate, w_up, w_down)):
+            set_block(
+                C_FF + 3 * start + part * chunk, dot(unit, weights[:, start : start + chunk])
+            )
     pl.semaphore_wait(barrier, 7)
 
     gathers = [
         Gather(number, whole, gather_send, gather_recv, me, coords)
         for number in range(len(PIECES))
     ]
-    order = (6, 7, 8, 3, 4, 5, 0, 1, 2)
-    for number in order:
-        gathers[number].step(0)
+
+    def gather(group, stage):
+        for number in range(3 * group, 3 * group + 3):
+            gathers[number].step(stage)
+
+    for group in range(GROUPS):
+        gather(group, 0)
 
     row = lax.broadcasted_iota(jnp.int32, (D, DP), 0)
     column = lax.broadcasted_iota(jnp.int32, (D, DP), 1)
     chosen = (column - column // PADDED == row) & (column % PADDED != SHARD)
     spread[...] = jnp.where(chosen, 1.0, 0.0).astype(BF)
-    own_rows = dot(rows_in[...], spread[...]).astype(BF)
+    own_rows = jnp.concatenate(
+        [dot_tn(rows_in[micro], spread[...]) for micro in range(MICRO)], axis=0
+    ).astype(BF)
 
     @pl.when(is_first)
     def _():
@@ -321,14 +372,28 @@
     def _():
         grad_out[...] = own_rows
 
-    for tick in range(1, 9):
-        for place in range(3):
-            stage = tick - place
-            if 1 <= stage <= 6:
-                for number in order[3 * place : 3 * place + 3]:
-                    gathers[number].step(stage)
-    for number in order:
-        gathers[number].finish()
+    for group in range(GROUPS):
+        gather(group, 1)
+
+    @pl.when(jnp.logical_not(is_first))
+    def _():
+        pl.semaphore_wait(turn, 1)
+
+    for stage in (2, 3):
+        for group in range(GROUPS):
+            gather(group, stage)
+    gather(0, 4)
+    gather(1, 4)
+    gather(0, 5)
+    gather(2, 4)
+    gather(1, 5)
+    gather(3, 4)
+
+    @pl.when(is_first)
+    def _():
+        pl.semaphore_signal(turn, inc=1, device_id={"section": 1 - section}, device_id_type=MESH)
+
+    gather(0, 6)
 
     def cross(target, slot):
         return pltpu.make_async_remote_copy(
@@ -343,17 +408,17 @@
     middle_copy = cross(entering, 0)
     grad_copy = cross(grad_out, 1)
 
-    @pl.when(jnp.logical_not(is_first))
-    def _():
-        middle_copy.wait_recv()
-
     picks = jnp.where(
         lax.broadcasted_iota(jnp.int32, (PADDED, DP), 1) % PADDED == SHARD, 1.0, 0.0
     ).astype(BF)
     gains[0:1, :] = dot(picks, columns(whole, C_Q, DP))[0:1]
-    gains[1:2, :] = dot(picks, columns(whole, C_G, DP))[0:1]
-    matrix = entering[...].astype(F32)
-    normed_one[...] = norm_forward(matrix, gains[0:1, :])
+    gains[1:2, :] = dot(picks, columns(whole, C_O, DP))[0:1]
+
+    @pl.when(jnp.logical_not(is_first))
+    def _():
+        middle_copy.wait_recv()
+
+    normed_one[...] = norm_forward(entering[...].astype(F32), gains[0:1, :])
 
     cos_rows = jnp.concatenate([cosine[...]] * MICRO, axis=0)
     sin_rows = jnp.concatenate([sine[...]] * MICRO, axis=0)
@@ -373,11 +438,13 @@
             part = turned if tile < 2 else jnp.where(low_lane, turned, part)
         key_value[:, tile * 128 : tile * 128 + 128] = part.astype(BF)
 
+    gather(2, 5)
+
     def attend(seq, carry):
         rows = pl.ds(pl.multiple_of(seq * SEQ, SEQ), SEQ)
         query_pos = lax.broadcasted_iota(jnp.int32, (GROUP, SEQ, SEQ), 1).reshape(GROUP * SEQ, SEQ)
         key_pos = lax.broadcasted_iota(jnp.int32, (GROUP * SEQ, SEQ), 1)
-        allowed = (key_pos <= query_pos) & (key_pos < lengths[seq, 0])
+        allowed = (key_pos <= query_pos) & (key_pos < lengths[0, seq])
         query_rows = queries[rows, :]
         kv_rows = key_value[rows, :]
         heads = []
@@ -399,64 +466,124 @@
         return carry
 
     lax.fori_loop(0, MICRO, attend, 0)
-    matrix = entering[...].astype(F32) + dot_nt(mixed[...], columns(whole, C_O, DP))
+    gather(3, 5)
+    inside = lax.broadcasted_iota(jnp.int32, (ROWS, DP), 1) % PADDED != SHARD
+    branch = jnp.where(inside, dot_nt(mixed[...], columns(whole, C_O, DP)), 0.0)
+    matrix = entering[...].astype(F32) + branch
     resid[...] = matrix
     normed_two[...] = norm_forward(matrix, gains[1:2, :])
     total[...] = matrix
 
-    def feed(step, carry):
-        at = pl.multiple_of(step * CHUNK, CHUNK)
-        here = pl.ds(at, CHUNK)
-        gates = dot(normed_two[...], columns(whole, C_G + at, CHUNK))
-        uppers = dot(normed_two[...], columns(whole, C_U + at, CHUNK))
-        gate_up[:, here] = gates.astype(BF)
-        gate_up[:, pl.ds(FF + at, CHUNK)] = uppers.astype(BF)
-        hiddens = (gates / (1.0 + jnp.exp(-gates)) * uppers).astype(BF)
-        hidden[:, here] = hiddens
-        total[...] += dot_nt(hiddens, columns(whole, C_D + at, CHUNK))
-        return carry
-
-    lax.fori_loop(0, CHUNKS, feed, 0)
-
-    def narrow(value):
+    def feed(chunk):
+        base = C_FF + 3 * STARTS[chunk]
+        width = CHUNKS[chunk]
+
+        def one(step, carry):
+            at = pl.multiple_of(step * SUB, SUB)
+            unit_at = pl.multiple_of(STARTS[chunk] + at, SUB)
+            gates = dot(normed_two[...], columns(whole, base + at, SUB))
+            uppers = dot(normed_two[...], columns(whole, base + width + at, SUB))
+            gate_up[:, pl.ds(unit_at, SUB)] = gates.astype(BF)
+            gate_up[:, pl.ds(FF + unit_at, SUB)] = uppers.astype(BF)
+            hiddens = (gates / (1.0 + jnp.exp(-gates)) * uppers).astype(BF)
+            hidden[:, pl.ds(unit_at, SUB)] = hiddens
+            total[...] += dot_nt(hiddens, columns(whole, base + 2 * width + at, SUB))
+            return carry
+
+        lax.fori_loop(0, width // SUB, one, 0)
+
+    for chunk in range(len(CHUNKS)):
+        gather(chunk + 1, 6)
+        feed(chunk)
+
+    def put_ends(value):
         high = value.astype(BF)
         low = (value - high.astype(F32)).astype(BF)
-        return dot_nt(high, spread[...]) + dot_nt(low, spread[...])
+        for micro in range(MICRO):
+            rows = slice(micro * SEQ, micro * SEQ + SEQ)
+            ends[micro] = dot_nt(spread[...], high[rows]) + dot_nt(spread[...], low[rows])
 
     @pl.when(is_first)
     def _():
         crossing[...] = total[...].astype(BF)
         middle_copy.start()
+
+    for piece in gathers:
+        piece.finish()
+
+    @pl.when(is_first)
+    def _():
         middle_copy.wait_send()
         grad_copy.wait_recv()
 
-    @pl.when(jnp.logical_not(is_first))
-    def _():
-        ends[...] = narrow(total[...])
-
-    total[...] = jnp.zeros_like(total)
-
-    def feed_back(step, carry):
-        at = pl.multiple_of(step * CHUNK, CHUNK)
-        here, beyond = pl.ds(at, CHUNK), pl.ds(FF + at, CHUNK)
-        grad_hidden = dot(grad_out[...], columns(whole, C_D + at, CHUNK))
-        gates = gate_up[:, here].astype(F32)
-        opened = 1.0 / (1.0 + jnp.exp(-gates))
-        grad_gate = (
-            grad_hidden * gate_up[:, beyond].astype(F32) * (opened * (1.0 + gates * (1.0 - opened)))
-        ).astype(BF)
-        grad_up = (grad_hidden * (gates * opened)).astype(BF)
-        gate_up[:, here] = grad_gate
-        gate_up[:, beyond] = grad_up
-        total[...] += dot_nt(grad_gate, columns(whole, C_G + at, CHUNK)) + dot_nt(
-            grad_up, columns(whole, C_U + at, CHUNK)
+    scatters = [
+        Scatter(
+            number,
+            whole,
+            [lands[6 * number + 2 * phase : 6 * number + 2 * phase + 2] for phase in range(3)],
+            scatter_send,
+            scatter_recv,
+            result,
+            me,
+            coords,
         )
-        return carry
-
-    lax.fori_loop(0, CHUNKS, feed_back, 0)
-    through, grad_gain = norm_backward(resid[...], gains[1:2, :], total[...])
-    grad_gains[...] = jnp.zeros_like(grad_gains)
-    grad_gains[1:2, 0:DP] = grad_gain
+        for number in range(len(PIECES))
+    ]
+    parts_of = ((0,), (1,), (2, 3), (4,), (5, 6), (7,), (8,))
+
+    def scatter(group, stage):
+        for part in parts_of[stage]:
+            for number in range(3 * group, 3 * group + 3):
+                scatters[number].step(part)
+
+    def put(left, right, first, count, gain=None):
+        grad = dot_tn(left, right)
+        if gain is not None:
+            at, gain_row = gain
+            row = lax.broadcasted_iota(jnp.int32, (DP, count), 0)
+            column = lax.broadcasted_iota(jnp.int32, (DP, count), 1) + at
+            own = (row % PADDED == SHARD) & (row // PADDED == column // PADDED)
+            grad = jnp.where(own, gain_row, grad)
+        whole[:, :, :, :, pl.ds(first, count)] = grad.astype(BF).reshape(4, 4, 4, PADDED, count)
+
+    total_back[...] = jnp.zeros_like(total_back)
+
+    def feed_back(chunk):
+        base = C_FF + 3 * STARTS[chunk]
+        width = CHUNKS[chunk]
+
+        def one(step, carry):
+            at = pl.multiple_of(step * SUB, SUB)
+            unit_at = pl.multiple_of(STARTS[chunk] + at, SUB)
+            grad_hidden = dot(grad_out[...], columns(whole, base + 2 * width + at, SUB))
+            gates = gate_up[:, pl.ds(unit_at, SUB)].astype(F32)
+            uppers = gate_up[:, pl.ds(FF + unit_at, SUB)].astype(F32)
+            opened = 1.0 / (1.0 + jnp.exp(-gates))
+            slope = opened * (1.0 + gates * (1.0 - opened))
+            grad_gate = (grad_hidden * uppers * slope).astype(BF)
+            grad_up = (grad_hidden * (gates * opened)).astype(BF)
+            total_back[...] += dot_nt(grad_gate, columns(whole, base + at, SUB)) + dot_nt(
+                grad_up, columns(whole, base + width + at, SUB)
+            )
+            put(normed_two[...], grad_gate, base + at, SUB)
+            put(normed_two[...], grad_up, base + width + at, SUB)
+            put(grad_out[...], hidden[:, pl.ds(unit_at, SUB)], base + 2 * width + at, SUB)
+            return carry
+
+        lax.fori_loop(0, width // SUB, one, 0)
+
+    feed_back(2)
+    scatter(3, 0)
+    feed_back(1)
+    scatter(2, 0)
+    scatter(3, 1)
+    feed_back(0)
+    scatter(1, 0)
+    scatter(3, 2)
+    scatter(2, 1)
+
+    through, grad_gain = norm_backward(resid[...], gains[1:2, :], total_back[...])
+    grad_gains[1:2, :] = grad_gain
     through = through + grad_out[...].astype(F32)
     grad_resid[...] = through
     grad_branch[...] = through.astype(BF)
@@ -489,14 +616,17 @@
             key_parts.append(dot_tn(grad_scores, query) * HD**-0.5)
             value_parts.append(dot_tn(chances.astype(BF), grad))
         query_parts.append(jnp.zeros((SEQ, HD), F32))
-        total[rows, :] = jnp.concatenate(query_parts, axis=1)
+        total_back[rows, :] = jnp.concatenate(query_parts, axis=1)
         grad_kv[rows, :] = jnp.concatenate(key_parts + value_parts, axis=1)
         return carry
 
     lax.fori_loop(0, MICRO, attend_back, 0)
+    scatter(3, 3)
+    scatter(2, 2)
+    scatter(1, 1)
     grad_query = grad_mixed
     for tile in range(8):
-        part = total[:, tile * 128 : tile * 128 + 128]
+        part = total_back[:, tile * 128 : tile * 128 + 128]
         grad_query[:, tile * 128 : tile * 128 + 128] = (
             part * cos_rows - swap_halves(part) * sin_rows
         ).astype(BF)
@@ -510,79 +640,54 @@
         key_value[...], columns(whole, C_KV, 640)
     )
     through, grad_gain = norm_backward(entering[...].astype(F32), gains[0:1, :], grad_normed)
-    grad_gains[0:1, 0:DP] = grad_gain
+    grad_gains[0:1, :] = grad_gain
     through = through + grad_resid[...]
 
     @pl.when(is_first)
     def _():
-        ends[...] = narrow(through)
+        total[...] = through
 
     @pl.when(jnp.logical_not(is_first))
     def _():
         crossing[...] = through.astype(BF)
         grad_copy.start()
+
+    for half in range(2):
+        at = half * SUB
+        here = slice(at, at + SUB)
+        put(normed_one[...], grad_query[:, here], C_Q + at, SUB, (at, grad_gains[0:1, here]))
+        put(grad_branch[...], mixed[:, here], C_O + at, SUB, (at, grad_gains[1:2, here]))
+    put(normed_one[...], key_value[...], C_KV, 640)
+    scatter(0, 0)
+    scatter(3, 4)
+    scatter(2, 3)
+    scatter(1, 2)
+    put_ends(total[...])
+    scatter(0, 1)
+    scatter(3, 5)
+    scatter(2, 4)
+    scatter(1, 3)
+    scatter(0, 2)
+    scatter(3, 6)
+    scatter(2, 5)
+    scatter(1, 4)
+    scatter(0, 3)
+    scatter(2, 6)
+    scatter(1, 5)
+    scatter(0, 4)
+    scatter(1, 6)
+    scatter(0, 5)
+    scatter(0, 6)
+    for slot, first in enumerate((C_Q, C_O)):
+        moved = pltpu.roll(result[SHARD, :, first : first + DP], DP - me * PADDED, 1)
+        gain_result[slot : slot + 1, :] = moved[:, 0:128]
+
+    @pl.when(jnp.logical_not(is_first))
+    def _():
         grad_copy.wait_send()
 
-    def put(left, right, first, count, gain):
-        grad = dot_tn(left, right)
-        if gain is not None:
-            at, gain_row = gain
-            row = lax.broadcasted_iota(jnp.int32, (DP, count), 0)
-            column = lax.broadcasted_iota(jnp.int32, (DP, count), 1) + at
-            own = (row % PADDED == SHARD) & (row // PADDED == column // PADDED)
-            grad = jnp.where(own, gain_row, grad)
-        whole[:, :, :, :, pl.ds(first, count)] = grad.astype(BF).reshape(4, 4, 4, PADDED, count)
-
-    number_of = len(PIECES)
-    scatters = [
-        Scatter(
-            number,
-            whole,
-            [lands[6 * number + 2 * phase : 6 * number + 2 * phase + 2] for phase in range(3)],
-            scatter_send,
-            scatter_recv,
-            result,
-            me,
-            coords,
-        )
-        for number in range(number_of)
-    ]
-
-    def put_down(step, carry):
-        at = pl.multiple_of(step * CHUNK, CHUNK)
-        put(grad_out[...], hidden[:, pl.ds(at, CHUNK)], C_D + at, CHUNK, None)
-        return carry
-
-    lax.fori_loop(0, CHUNKS, put_down, 0)
-    for number in (0, 1, 2):
-        scatters[number].step(0)
-
-    def put_gate_up(step, carry):
-        at = pl.multiple_of(step * CHUNK, CHUNK)
-        gain = (at, grad_gains[1:2, pl.ds(at, CHUNK)])
-        put(normed_two[...], gate_up[:, pl.ds(at, CHUNK)], C_G + at, CHUNK, gain)
-        return carry
-
-    lax.fori_loop(0, 2 * CHUNKS, put_gate_up, 0)
-    for number in (3, 4, 5):
-        scatters[number].step(0)
-    for half in range(2):
-        at = half * CHUNK
-        gain = (at, grad_gains[0:1, at : at + CHUNK])
-        put(normed_one[...], grad_query[:, at : at + CHUNK], C_Q + at, CHUNK, gain)
-        put(grad_branch[...], mixed[:, at : at + CHUNK], C_O + at, CHUNK, None)
-    put(normed_one[...], key_value[...], C_KV, 640, None)
-    for number in (6, 7, 8):
-        scatters[number].step(0)
-
-    for tick in range(1, 11):
-        for place in range(3):
-            stage = tick - place
-            if 1 <= stage <= 8:
-                for number in range(3 * place, 3 * place + 3):
-                    scatters[number].step(stage)
-    for number in range(number_of):
-        scatters[number].finish()
+    for piece in scatters:
+        piece.finish()
 
 
 def rope_tables():
@@ -595,7 +700,7 @@
     )
 
 
-def run_kernel(shard, rows_in, lengths, cosine, sine):
+def run_kernel(weights, gain_attn, gain_mlp, rows_in, lengths, cosine, sine):
     scratch = [
         ((RING, RING, RING, PADDED, C_ALL), BF),
         ((ROWS, DP), BF),
@@ -613,11 +718,12 @@
         ((ROWS, FF), BF),
         ((ROWS, DP), F32),
         ((ROWS, DP), F32),
+        ((ROWS, DP), F32),
         ((ROWS, DP), BF),
         ((ROWS, DP), BF),
         ((ROWS, 640), F32),
         ((8, DP), F32),
-        ((8, 2 * FF), F32),
+        ((8, DP), F32),
     ]
     scratch = [pltpu.VMEM(shape, kind) for shape, kind in scratch]
     count = len(PIECES)
@@ -628,8 +734,9 @@
         pltpu.SemaphoreType.DMA((count, 18)),
         pltpu.SemaphoreType.DMA((2,)),
         pltpu.SemaphoreType.DMA((2,)),
+        pltpu.SemaphoreType.REGULAR,
     ]
-    for first, mid, last, _ in PIECES:
+    for first, mid, last, _, _ in PIECES:
         for phase in range(3):
             for width in (mid - first, last - mid):
                 shape = (3,) + (RING,) * (2 - phase) + (PADDED, width)
@@ -638,75 +745,51 @@
     return pl.pallas_call(
         kernel,
         out_shape=(
-            jax.ShapeDtypeStruct((ROWS, D), F32),
-            jax.ShapeDtypeStruct((PADDED, C_ALL), F32),
+            jax.ShapeDtypeStruct((MICRO, D, SEQ), F32),
+            jax.ShapeDtypeStruct((PADDED, 1, C_ALL), F32),
+            jax.ShapeDtypeStruct((2, 128), F32),
         ),
-        in_specs=[vmem, vmem, pl.BlockSpec(memory_space=pltpu.SMEM), vmem, vmem],
-        out_specs=(vmem, vmem),
+        in_specs=[vmem] * 10 + [pl.BlockSpec(memory_space=pltpu.SMEM), vmem, vmem],
+        out_specs=(vmem, vmem, vmem),
         scratch_shapes=scratch,
         compiler_params=pltpu.CompilerParams(
             collective_id=0, has_side_effects=True, vmem_limit_bytes=64 * 1024 * 1024
         ),
-    )(shard, rows_in, lengths, cosine, sine)
+    )(*weights, gain_attn, gain_mlp, rows_in, lengths, cosine, sine)
 
 
 def local(
     boundary, lengths, gain_attn, w_query, w_key, w_value, w_out, gain_mlp, w_gate, w_up, w_down
 ):
-    me = lax.axis_index("dp")
-
-    def pad(matrix, width):
-        return jnp.pad(matrix, ((0, 0), (0, width - matrix.shape[1])))
-
-    body = jnp.concatenate(
-        [
-            pad(w_query[0], 1024),
-            pad(w_out[0].T, 1024),
-            w_key[0],
-            w_value[0],
-            w_gate[0],
-            w_up[0],
-            w_down[0].T,
-        ],
-        axis=1,
-    )
-    ours = jnp.arange(DP // PADDED)[:, None] == me
-    spread_one = jnp.where(ours, pad(gain_attn, PADDED), 0).reshape(1, DP)
-    spread_two = jnp.where(ours, pad(gain_mlp, PADDED), 0).reshape(1, DP)
-    last = jnp.concatenate(
-        [
-            spread_one,
-            jnp.zeros((1, C_G - DP), BF),
-            spread_two,
-            jnp.zeros((1, C_ALL - C_G - DP), BF),
-        ],
-        axis=1,
-    )
-    shard = jnp.concatenate([body, last.astype(BF)], axis=0)
     cosine, sine = rope_tables()
-    ends, result = run_kernel(
-        shard,
-        boundary[0].reshape(ROWS, D),
-        lengths,
+    weights = (w_query[0], w_out[0].T, w_key[0], w_value[0], w_gate[0], w_up[0], w_down[0].T)
+    ends, result, gains = run_kernel(
+        weights,
+        gain_attn,
+        gain_mlp,
+        boundary[0].transpose(0, 2, 1),
+        lengths.T,
         jnp.asarray(cosine),
         jnp.asarray(sine),
     )
-    body = result[:SHARD]
-
-    def gain_of(first):
-        return result[SHARD, first : first + DP].reshape(DP // PADDED, PADDED).sum(axis=0)[:SHARD]
+
+    def rows(first, count):
+        return result[:SHARD, :, first : first + count].transpose(1, 0, 2)
+
+    def turned(first, count):
+        return result[:SHARD, :, first : first + count].transpose(1, 2, 0)
 
     return (
-        ends.reshape(1, MICRO, SEQ, D),
-        gain_of(C_Q)[None],
-        body[None, :, C_Q : C_Q + D],
-        body[None, :, C_KV : C_KV + 320],
-        body[None, :, C_KV + 320 : C_KV + 640],
-        body[:, C_O : C_O + D].T[None],
-        gain_of(C_G)[None],
-        body[None, :, C_G : C_G + FF],
-        body[None, :, C_U : C_U + FF],
-        body[:, C_D : C_D + FF].T[None],
+        ends.transpose(0, 2, 1)[None],
+        gains[0:1, :SHARD],
+        rows(C_Q, D),
+        rows(C_KV, 320),
+        rows(C_KV + 320, 320),
+        turned(C_O, D),
+        gains[1:2, :SHARD],
+        rows(C_FF, FF),
+        rows(C_FF + FF, FF),
+        turned(C_FF + 2 * FF, FF),
     )
 
 

time: 253 us -> 208 us (0.82)
  Pallas kernels: 234 us -> 200 us
  local copies, waits for them, and re-layouts: 16.4 us -> 7.1 us
    pallas_call x1, Pallas kernels: 234 us -> 200 us  [run_kernel(): pl.pallas_call(kernel, out_shape=(jax.ShapeDtypeStruct((MICRO, D, SEQ), F...]
    unnamed x24 -> x5, local copies, waits for them, and re-layouts: 9.68 us -> 1.61 us
    transpose x0 -> x3, local copies, waits for them, and re-layouts: none -> 4.97 us  [the longest x2 3.44 us: turned(): return result[:SHARD, :, first:first + count].transpose(1, 2, 0)]
    broadcast_in_dim x8 -> x0, local copies, waits for them, and re-layouts: 4.61 us -> none  [the longest x1 1.11 us: local(): body[:, C_D:C_D + FF].T[None]]
where the time goes in v2:
time: 208 us; the launch traced here: 207 us
  Pallas kernels  200 us (96%)
  local copies, waits for them, and re-layouts  7.1 us (3%)
    pallas_call x1, Pallas kernels, run_kernel(): pl.pallas_call(kernel, out_shape=(jax.ShapeDtypeStruct((MICRO, D, SEQ), F...  200 us

profile of v2, /device:TPU:0, one launch (start us, length us, event | category | flops | bytes accessed | tf_op | source)
XLA Modules:
  0.0 207.3 jit_solution(9735750216256215523)
XLA Ops:
  0.6 199.5 %shard_map.204 = (f32[2,960,128]{2,1,0:T(8,128)}, f32[16,1,10368]{2,1,0:T(1,128)}, f32[2,128]{1,0:T(2,128)}) custom-call(bf16[15,960]{1,0:T(8,128)(2,1)} %bitcast.37, bf16[15,960]{1,0:T(8,128)(2,1)} %bitcast.38, bf16[15,320]{1,0:T(8,128)(2,1)} %bitcast.39, bf16[15,320]{1,0:T(8,128)(2,1)} %bitcast.40, bf16[15,2560]{1,0:T(8,128)(2,1)} %bitcast.34, ...), custom_call_target="tpu_custom_call" | custom-call | tf_op jit(solution)/shard_map/pallas_call | solution.py:745
  200.2 0.0 copy-start
  200.2 1.9 slice_bitcast_fusion
  202.1 1.5 slice_bitcast_fusion.3
  203.6 1.5 slice_bitcast_fusion.5
  205.1 0.0 copy-start.1
  205.2 0.7 copy-done.1
  205.8 0.5 fusion
  206.3 0.0 copy-done
  206.3 0.9 copy.24
Async XLA Ops:
  200.2 6.2 %copy-start = (f32[2,960,128]{2,1,0:T(8,128)S(1)}, f32[2,960,128]{2,1,0:T(8,128)}, u32[]{:S(2)}) copy-start(f32[2,960,128]{2,1,0:T(8,128)} %get-tuple-element.13) | copy-start | bytes 2949124
  205.1 0.7 copy-start.1

commit v3 on v2

v3 whole, which is shorter than its diff:
```python
import numpy as np

import jax
import jax.numpy as jnp
from jax import lax
from jax.experimental import pallas as pl
from jax.experimental.pallas import tpu as pltpu
from jax.sharding import PartitionSpec as P

D = 960
DP = 1024
HQ = 15
KV = 5
GROUP = HQ // KV
HD = 64
FF = 2560
SEQ = 128
MICRO = 2
ROWS = MICRO * SEQ
RING = 4
SHARD = 15
PADDED = 16
EPS = 1e-05
NEG = -1e30
BASE = 10000.0
BF = jnp.bfloat16
F32 = jnp.float32
MESH = pl.DeviceIdType.MESH

C_Q = 0
C_KV = 1024
C_O = 1664
C_FF = 2688
C_ALL = C_FF + 3 * FF
SUB = 512

STRIDES = (16, 4, 1)
ORDERS = ((0, 1, 2), (1, 2, 0), (2, 0, 1))

CHUNKS = ((0, 1024), (1024, 2048), (2048, 2560))
LARGE = [
    [(0, 512, 896, 0), (896, 1280, 1664, 1)],
    [(1664, 1792, 1792, 1), (1792, 2304, 2688, 2)],
] + [
    [
        (C_FF + FF * part + first, C_FF + FF * part + (first + last) // 2, C_FF + FF * part + last, part)
        for part in range(3)
    ]
    for first, last in CHUNKS
]
GROUPS = len(LARGE)
MERGED = [
    [(896 * part, 896 * part + 512, 896 * part + 896, part) for part in range(3)],
    [
        (C_FF + FF * part, C_FF + FF * part + FF // 2, C_FF + FF * part + FF, part)
        for part in range(3)
    ],
]


def position():
    me = lax.axis_index("dp")
    return me, (me // 16, (me // 4) % 4, me % 4)


def neighbour(me, coords, axis, step):
    here = coords[axis]
    return me + ((here + step) % RING - here) * STRIDES[axis]


def remote(src, dst, send, recv, device):
    return pltpu.make_async_remote_copy(
        src_ref=src,
        dst_ref=dst,
        send_sem=send,
        recv_sem=recv,
        device_id={"dp": device},
        device_id_type=MESH,
    )


class Ring:
    def __init__(self, piece, phase, later_full, whole, sems, me, coords):
        self.first, self.mid, self.last, part = piece
        self.order, self.phase, self.later_full = ORDERS[part], phase, later_full
        self.axis = self.order[phase]
        self.whole, self.sems = whole, sems
        self.me, self.coords = me, coords
        self.near = neighbour(me, coords, self.axis, 1)
        here = coords[self.axis]
        self.here, self.ahead, self.across, self.behind = [
            (here + step) % RING for step in range(4)
        ]

    def span(self, side):
        return ((self.first, self.last), (self.first, self.mid), (self.mid, self.last))[side]

    def view(self, at, side=0):
        first, last = self.span(side)
        index = [None, None, None]
        for place, axis in enumerate(self.order):
            if place == self.phase:
                index[axis] = at
            elif (place > self.phase) == self.later_full:
                index[axis] = slice(None)
            else:
                index[axis] = self.coords[axis]
        return self.whole.at[index[0], index[1], index[2], :, first:last]

    def widths(self):
        return [side for side in (1, 2) if self.span(side)[0] < self.span(side)[1]]

    def copy(self, src, dst, send, recv, step):
        remote(
            src,
            dst,
            self.sems.at[send],
            self.sems.at[recv],
            neighbour(self.me, self.coords, self.axis, step),
        ).start()

    def wait_recv(self, ref, sem):
        remote(ref, ref, self.sems.at[sem], self.sems.at[sem], self.near).wait_recv()

    def wait_send(self, ref, sem):
        remote(ref, ref, self.sems.at[sem], self.sems.at[sem], self.near).wait_send()


class DirectGather(Ring):
    count = 2

    def go(self):
        view = self.view(self.here)
        for step in (1, -1, 2):
            self.copy(view, view, 0, 1, step)

    def done(self):
        self.wait_recv(self.view(slice(0, 3)), 1)

    def finish(self):
        self.wait_send(self.view(slice(0, 3)), 0)


class RingGather(Ring):
    count = 3

    def go(self):
        view = self.view(self.here)
        self.copy(view, view, 0, 1, 1)
        self.copy(view, view, 0, 1, -1)

    def forward(self):
        self.wait_recv(self.view(slice(0, 2)), 1)
        sides = self.widths()
        right = self.view(self.behind, 1)
        self.copy(right, right, 0, 2, 1)
        if 2 in sides:
            left = self.view(self.ahead, 2)
            self.copy(left, left, 0, 2, -1)

    def done(self):
        self.wait_recv(self.view(self.here), 2)

    def finish(self):
        self.wait_send(self.view(slice(0, 3)), 0)


class DirectScatter(Ring):
    count = 2

    def __init__(self, *args, lands, result=None):
        super().__init__(*args)
        (self.land,), self.result = lands, result

    def go(self):
        for slot, step in enumerate((1, -1, 2)):
            at = (self.ahead, self.behind, self.across)[slot]
            self.copy(self.view(at), self.land.at[slot], 0, 1, step)

    def done(self):
        self.wait_recv(self.land, 1)
        view = self.view(self.here)
        if self.result is not None:
            total = view[...].astype(F32)
            for slot in range(3):
                total = total + self.land[slot].astype(F32)
            self.result(self.first, self.last, total)
            return

        def one(step, carry):
            total = view[step].astype(F32)
            for slot in range(3):
                total = total + self.land[slot, step].astype(F32)
            view[step] = total.astype(BF)
            return carry

        lax.fori_loop(0, RING, one, 0)

    def finish(self):
        self.wait_send(self.land, 0)


class RingScatter(Ring):
    count = 6

    def __init__(self, *args, lands):
        super().__init__(*args)
        self.lands = dict(zip(self.widths(), lands))

    def send(self, side, slot, at, step):
        base = 3 * (side - 1)
        self.copy(
            self.view(at, side), self.lands[side].at[slot], base, base + (1 if slot == 0 else 2), step
        )

    def add(self, at, side, slots):
        view, land = self.view(at, side), self.lands[side]

        def one(step, carry):
            total = view[step].astype(F32)
            for slot in slots:
                total = total + land[slot, step].astype(F32)
            view[step] = total.astype(BF)
            return carry

        lax.fori_loop(0, RING, one, 0)

    def go(self):
        sides = self.widths()
        self.send(1, 0, self.across, 1)
        if 2 in sides:
            self.send(2, 0, self.across, -1)
            self.send(2, 1, self.ahead, 1)
        self.send(1, 1, self.behind, -1)

    def forward(self):
        for side in self.widths():
            step, at = ((1, self.ahead), (-1, self.behind))[side - 1]
            self.wait_recv(self.lands[side].at[0], 3 * (side - 1) + 1)
            self.add(at, side, (0,))
            self.send(side, 2, at, step)

    def done(self):
        for side in self.widths():
            self.wait_recv(self.lands[side].at[1:3], 3 * (side - 1) + 2)
            self.add(self.here, side, (1, 2))

    def finish(self):
        for side in self.widths():
            self.wait_send(self.lands[side], 3 * (side - 1))


PLAN = {}
LANDS = []
SEMS = 0
for kind, cls, pieces, phase in (
    ("g1", DirectGather, MERGED, 0),
    ("g2", RingGather, MERGED, 1),
    ("g3", RingGather, LARGE, 2),
    ("s1", RingScatter, LARGE, 0),
    ("s2", DirectScatter, MERGED[:1], 1),
    ("s2", RingScatter, MERGED[1:], 1),
    ("s3", DirectScatter, MERGED, 2),
):
    for group in pieces:
        entries = []
        for piece in group:
            mine = []
            first, mid, last, _ = piece
            if cls is DirectScatter:
                mine = [last - first]
            elif cls is RingScatter:
                mine = [width for width in (mid - first, last - mid) if width]
            for width in mine:
                LANDS.append((3,) + (RING,) * (2 - phase) + (PADDED, width))
            entries.append((cls, piece, phase, SEMS, len(LANDS) - len(mine), len(LANDS)))
            SEMS += cls.count
        PLAN.setdefault(kind, []).append(entries)


def dot(left, right):
    return jnp.dot(left, right, preferred_element_type=F32)


def dot_nt(left, right):
    return lax.dot_general(left, right, (((1,), (1,)), ((), ())), preferred_element_type=F32)


def dot_tn(left, right):
    return lax.dot_general(left, right, (((0,), (0,)), ((), ())), preferred_element_type=F32)


def columns(whole, first, count):
    return whole[:, :, :, :, pl.ds(first, count)].reshape(DP, count)


def swap_halves(tile):
    lane = lax.broadcasted_iota(jnp.int32, tile.shape, 1)
    return jnp.where(lane % HD < HD // 2, pltpu.roll(tile, 96, 1), pltpu.roll(tile, 32, 1))


def norm_forward(matrix, gain):
    scale = lax.rsqrt(jnp.sum(matrix * matrix, axis=1, keepdims=True) * (1.0 / D) + EPS)
    return (matrix * scale * gain).astype(BF)


def norm_backward(matrix, gain, grad):
    scale = lax.rsqrt(jnp.sum(matrix * matrix, axis=1, keepdims=True) * (1.0 / D) + EPS)
    scaled = grad * gain
    inner = jnp.sum(scaled * matrix, axis=1, keepdims=True) * (1.0 / D)
    grad_matrix = scale * (scaled - matrix * (scale * scale * inner))
    grad_gain = jnp.sum(grad * matrix * scale, axis=0, keepdims=True)
    return grad_matrix, grad_gain


def kernel(
    w_query,
    w_out,
    w_key,
    w_value,
    w_gate,
    w_up,
    w_down,
    gain_attn,
    gain_mlp,
    rows_in,
    lengths,
    cosine,
    sine,
    ends,
    grad_w_query,
    grad_w_key,
    grad_w_value,
    grad_w_out,
    grad_w_gate,
    grad_w_up,
    grad_w_down,
    grad_gain_attn,
    grad_gain_mlp,
    whole,
    entering,
    grad_out,
    crossing,
    spread,
    normed_one,
    queries,
    key_value,
    probs,
    mixed,
    resid,
    normed_two,
    gate_up,
    hidden,
    total,
    total_back,
    grad_resid,
    grad_branch,
    grad_mixed,
    grad_kv,
    gains,
    grad_gains,
    sems,
    cross_send,
    cross_recv,
    turn,
    *lands,
):
    section = lax.axis_index("section")
    me, coords = position()
    is_first = section == 0

    barrier = pltpu.get_barrier_semaphore()
    for axis in range(3):
        for step in (1, -1, 2):
            pl.semaphore_signal(
                barrier,
                inc=1,
                device_id={"dp": neighbour(me, coords, axis, step)},
                device_id_type=MESH,
            )
    pl.semaphore_signal(barrier, inc=1, device_id={"section": 1 - section}, device_id_type=MESH)

    unit = jnp.where(
        lax.broadcasted_iota(jnp.int32, (PADDED, SHARD), 0)
        == lax.broadcasted_iota(jnp.int32, (PADDED, SHARD), 1),
        1.0,
        0.0,
    ).astype(BF)
    place = jnp.where(
        lax.broadcasted_iota(jnp.int32, (SHARD, DP), 1)
        == lax.broadcasted_iota(jnp.int32, (SHARD, DP), 0) + me * PADDED,
        1.0,
        0.0,
    ).astype(BF)
    last_row = lax.broadcasted_iota(jnp.int32, (PADDED, DP), 0) == SHARD

    def set_block(first, value):
        whole[coords[0], coords[1], coords[2], :, first : first + value.shape[1]] = value.astype(BF)

    def with_gain(weights, gain):
        body = jnp.concatenate(
            [dot(unit, weights[...]), jnp.zeros((PADDED, DP - D), F32)], axis=1
        )
        return jnp.where(last_row, dot(gain[...], place), body)

    set_block(C_Q, with_gain(w_query, gain_attn))
    set_block(C_O, with_gain(w_out, gain_mlp))
    set_block(C_KV, jnp.concatenate([dot(unit, w_key[...]), dot(unit, w_value[...])], axis=1))
    for part, weights in enumerate((w_gate, w_up, w_down)):
        set_block(C_FF + FF * part, dot(unit, weights[...]))
    pl.semaphore_wait(barrier, 10)

    homes = (
        (C_Q, D, grad_w_query),
        (C_KV, 320, grad_w_key),
        (C_KV + 320, 320, grad_w_value),
        (C_O, D, grad_w_out),
        (C_FF, FF, grad_w_gate),
        (C_FF + FF, FF, grad_w_up),
        (C_FF + 2 * FF, FF, grad_w_down),
    )

    def put_result(first, last, value):
        for start, count, ref in homes:
            low, high = max(first, start), min(last, start + count)
            if low < high:
                for row in range(SHARD):
                    ref[row, :, low - start : high - start] = value[
                        row : row + 1, low - first : high - first
                    ]
        for slot, start in enumerate((C_Q, C_O)):
            low, high = max(first, start), min(last, start + DP)
            if low < high:
                grad_gains[2 + slot : 3 + slot, low - start : high - start] = value[
                    SHARD : SHARD + 1, low - first : high - first
                ]

    started = []

    def make(entry):
        cls, piece, phase, sem, land, land_end = entry
        args = (piece, phase, cls in (RingScatter, DirectScatter), whole)
        args += (sems.at[sem : sem + cls.count], me, coords)
        if cls is DirectScatter:
            made = cls(
                *args, lands=lands[land:land_end], result=put_result if phase == 2 else None
            )
        elif cls is RingScatter:
            made = cls(*args, lands=lands[land:land_end])
        else:
            made = cls(*args)
        started.append(made)
        return made

    transfers = {
        kind: [[make(entry) for entry in group] for group in groups]
        for kind, groups in PLAN.items()
    }
    gathers = [made for made in started if isinstance(made, (DirectGather, RingGather))]
    scatters = [made for made in started if isinstance(made, (DirectScatter, RingScatter))]

    def run(kind, group, act):
        for made in transfers[kind][group]:
            getattr(made, act)()

    run("g1", 0, "go")
    run("g1", 1, "go")

    row = lax.broadcasted_iota(jnp.int32, (D, DP), 0)
    column = lax.broadcasted_iota(jnp.int32, (D, DP), 1)
    chosen = (column - column // PADDED == row) & (column % PADDED != SHARD)
    spread[...] = jnp.where(chosen, 1.0, 0.0).astype(BF)
    own_rows = jnp.concatenate(
        [dot_tn(rows_in[micro], spread[...]) for micro in range(MICRO)], axis=0
    ).astype(BF)

    @pl.when(is_first)
    def _():
        entering[...] = own_rows

    @pl.when(jnp.logical_not(is_first))
    def _():
        grad_out[...] = own_rows

    for group in range(2):
        run("g1", group, "done")
        run("g2", group, "go")

    def hand_over():
        @pl.when(is_first)
        def _():
            pl.semaphore_signal(
                turn, inc=1, device_id={"section": 1 - section}, device_id_type=MESH
            )

    def take_over():
        @pl.when(jnp.logical_not(is_first))
        def _():
            pl.semaphore_wait(turn, 1)

    for group in range(2):
        run("g2", group, "forward")
    run("g2", 0, "done")
    take_over()
    run("g3", 0, "go")
    run("g3", 1, "go")
    run("g2", 1, "done")
    run("g3", 2, "go")
    run("g3", 0, "forward")
    run("g3", 3, "go")
    run("g3", 1, "forward")
    run("g3", 4, "go")
    run("g3", 2, "forward")
    run("g3", 0, "done")

    def cross(target, slot):
        return pltpu.make_async_remote_copy(
            src_ref=crossing,
            dst_ref=target,
            send_sem=cross_send.at[slot],
            recv_sem=cross_recv.at[slot],
            device_id={"section": 1 - section},
            device_id_type=MESH,
        )

    middle_copy = cross(entering, 0)
    grad_copy = cross(grad_out, 1)

    picks = jnp.where(
        lax.broadcasted_iota(jnp.int32, (PADDED, DP), 1) % PADDED == SHARD, 1.0, 0.0
    ).astype(BF)
    gains[0:1, :] = dot(picks, columns(whole, C_Q, DP))[0:1]

    @pl.when(jnp.logical_not(is_first))
    def _():
        middle_copy.wait_recv()

    normed_one[...] = norm_forward(entering[...].astype(F32), gains[0:1, :])

    cos_rows = jnp.concatenate([cosine[...]] * MICRO, axis=0)
    sin_rows = jnp.concatenate([sine[...]] * MICRO, axis=0)
    low_lane = lax.broadcasted_iota(jnp.int32, (ROWS, 128), 1) < HD

    for half in range(2):
        pre = dot(normed_one[...], columns(whole, C_Q + half * 512, 512))
        for tile in range(4):
            part = pre[:, tile * 128 : tile * 128 + 128]
            at = half * 512 + tile * 128
            queries[:, at : at + 128] = (part * cos_rows + swap_halves(part) * sin_rows).astype(BF)
    pre = dot(normed_one[...], columns(whole, C_KV, 640))
    for tile in range(5):
        part = pre[:, tile * 128 : tile * 128 + 128]
        if tile < 3:
            turned = part * cos_rows + swap_halves(part) * sin_rows
            part = turned if tile < 2 else jnp.where(low_lane, turned, part)
        key_value[:, tile * 128 : tile * 128 + 128] = part.astype(BF)

    def attend(seq, carry):
        rows = pl.ds(pl.multiple_of(seq * SEQ, SEQ), SEQ)
        query_pos = lax.broadcasted_iota(jnp.int32, (GROUP, SEQ, SEQ), 1).reshape(GROUP * SEQ, SEQ)
        key_pos = lax.broadcasted_iota(jnp.int32, (GROUP * SEQ, SEQ), 1)
        allowed = (key_pos <= query_pos) & (key_pos < lengths[0, seq])
        query_rows = queries[rows, :]
        kv_rows = key_value[rows, :]
        heads = []
        for group in range(KV):
            at = group * GROUP * HD
            query = jnp.concatenate(
                [query_rows[:, at + h * HD : at + h * HD + HD] for h in range(GROUP)], axis=0
            )
            key = kv_rows[:, group * HD : group * HD + HD]
            value = kv_rows[:, (KV + group) * HD : (KV + group) * HD + HD]
            scores = jnp.where(allowed, dot_nt(query, key) * HD**-0.5, NEG)
            expos = jnp.exp(scores - jnp.max(scores, axis=1, keepdims=True))
            chances = expos / jnp.sum(expos, axis=1, keepdims=True)
            probs[seq, group] = chances
            out = dot(chances.astype(BF), value)
            heads.extend(out[h * SEQ : h * SEQ + SEQ] for h in range(GROUP))
        heads.append(jnp.zeros((SEQ, HD), F32))
        mixed[rows, :] = jnp.concatenate(heads, axis=1).astype(BF)
        return carry

    lax.fori_loop(0, MICRO, attend, 0)
    run("g3", 3, "forward")
    run("g3", 1, "done")
    gains[1:2, :] = dot(picks, columns(whole, C_O, DP))[0:1]
    inside = lax.broadcasted_iota(jnp.int32, (ROWS, DP), 1) % PADDED != SHARD
    branch = jnp.where(inside, dot_nt(mixed[...], columns(whole, C_O, DP)), 0.0)
    matrix = entering[...].astype(F32) + branch
    resid[...] = matrix
    normed_two[...] = norm_forward(matrix, gains[1:2, :])
    total[...] = matrix
    run("g3", 4, "forward")
    hand_over()

    def feed(chunk):
        def one(step, carry):
            unit_at = pl.multiple_of(step * SUB, SUB)
            gates = dot(normed_two[...], columns(whole, C_FF + unit_at, SUB))
            uppers = dot(normed_two[...], columns(whole, C_FF + FF + unit_at, SUB))
            gate_up[:, pl.ds(unit_at, SUB)] = gates.astype(BF)
            gate_up[:, pl.ds(FF + unit_at, SUB)] = uppers.astype(BF)
            hiddens = (gates / (1.0 + jnp.exp(-gates)) * uppers).astype(BF)
            hidden[:, pl.ds(unit_at, SUB)] = hiddens
            total[...] += dot_nt(hiddens, columns(whole, C_FF + 2 * FF + unit_at, SUB))
            return carry

        first, last = CHUNKS[chunk]
        lax.fori_loop(first // SUB, last // SUB, one, 0)

    for chunk in range(len(CHUNKS)):
        run("g3", chunk + 2, "done")
        feed(chunk)

    def put_ends(value):
        high = value.astype(BF)
        low = (value - high.astype(F32)).astype(BF)
        for micro in range(MICRO):
            rows = slice(micro * SEQ, micro * SEQ + SEQ)
            ends[micro] = dot_nt(spread[...], high[rows]) + dot_nt(spread[...], low[rows])

    @pl.when(is_first)
    def _():
        crossing[...] = total[...].astype(BF)
        middle_copy.start()

    for made in gathers:
        made.finish()

    @pl.when(is_first)
    def _():
        middle_copy.wait_send()
        grad_copy.wait_recv()

    def put(left, right, first, count, gain=None):
        grad = dot_tn(left, right)
        if gain is not None:
            at, gain_row = gain
            row = lax.broadcasted_iota(jnp.int32, (DP, count), 0)
            column = lax.broadcasted_iota(jnp.int32, (DP, count), 1) + at
            own = (row % PADDED == SHARD) & (row // PADDED == column // PADDED)
            grad = jnp.where(own, gain_row, grad)
        whole[:, :, :, :, pl.ds(first, count)] = grad.astype(BF).reshape(4, 4, 4, PADDED, count)

    total_back[...] = jnp.zeros_like(total_back)

    def feed_back(chunk):
        def one(step, carry):
            unit_at = pl.multiple_of(step * SUB, SUB)
            gate_at, up_at, down_at = [C_FF + FF * part + unit_at for part in range(3)]
            grad_hidden = dot(grad_out[...], columns(whole, down_at, SUB))
            gates = gate_up[:, pl.ds(unit_at, SUB)].astype(F32)
            uppers = gate_up[:, pl.ds(FF + unit_at, SUB)].astype(F32)
            opened = 1.0 / (1.0 + jnp.exp(-gates))
            slope = opened * (1.0 + gates * (1.0 - opened))
            grad_gate = (grad_hidden * uppers * slope).astype(BF)
            grad_up = (grad_hidden * (gates * opened)).astype(BF)
            total_back[...] += dot_nt(grad_gate, columns(whole, gate_at, SUB)) + dot_nt(
                grad_up, columns(whole, up_at, SUB)
            )
            put(normed_two[...], grad_gate, gate_at, SUB)
            put(normed_two[...], grad_up, up_at, SUB)
            put(grad_out[...], hidden[:, pl.ds(unit_at, SUB)], down_at, SUB)
            return carry

        first, last = CHUNKS[chunk]
        lax.fori_loop(first // SUB, last // SUB, one, 0)

    feed_back(2)
    run("s1", 4, "go")
    feed_back(1)
    run("s1", 3, "go")
    feed_back(0)
    run("s1", 2, "go")

    through, grad_gain = norm_backward(resid[...], gains[1:2, :], total_back[...])
    grad_gains[1:2, :] = grad_gain
    through = through + grad_out[...].astype(F32)
    grad_resid[...] = through
    grad_branch[...] = through.astype(BF)
    grad_mixed[...] = dot(grad_branch[...], columns(whole, C_O, DP)).astype(BF)
    for half in range(2):
        at = half * SUB
        here = slice(at, at + SUB)
        put(grad_branch[...], mixed[:, here], C_O + at, SUB, (at, grad_gains[1:2, here]))
    run("s1", 1, "go")
    run("s1", 4, "forward")

    def attend_back(seq, carry):
        rows = pl.ds(pl.multiple_of(seq * SEQ, SEQ), SEQ)
        query_rows = queries[rows, :]
        kv_rows = key_value[rows, :]
        grad_rows = grad_mixed[rows, :]
        query_parts = []
        key_parts = []
        value_parts = []
        for group in range(KV):
            at = group * GROUP * HD
            query = jnp.concatenate(
                [query_rows[:, at + h * HD : at + h * HD + HD] for h in range(GROUP)], axis=0
            )
            grad = jnp.concatenate(
                [grad_rows[:, at + h * HD : at + h * HD + HD] for h in range(GROUP)], axis=0
            )
            key = kv_rows[:, group * HD : group * HD + HD]
            value = kv_rows[:, (KV + group) * HD : (KV + group) * HD + HD]
            chances = probs[seq, group]
            grad_probs = dot_nt(grad, value)
            inner = jnp.sum(chances * grad_probs, axis=1, keepdims=True)
            grad_scores = (chances * (grad_probs - inner)).astype(BF)
            grad_query = dot(grad_scores, key) * HD**-0.5
            query_parts.extend(grad_query[h * SEQ : h * SEQ + SEQ] for h in range(GROUP))
            key_parts.append(dot_tn(grad_scores, query) * HD**-0.5)
            value_parts.append(dot_tn(chances.astype(BF), grad))
        query_parts.append(jnp.zeros((SEQ, HD), F32))
        total_back[rows, :] = jnp.concatenate(query_parts, axis=1)
        grad_kv[rows, :] = jnp.concatenate(key_parts + value_parts, axis=1)
        return carry

    lax.fori_loop(0, MICRO, attend_back, 0)
    run("s1", 3, "forward")
    grad_query = grad_mixed
    for tile in range(8):
        part = total_back[:, tile * 128 : tile * 128 + 128]
        grad_query[:, tile * 128 : tile * 128 + 128] = (
            part * cos_rows - swap_halves(part) * sin_rows
        ).astype(BF)
    for tile in range(5):
        part = grad_kv[:, tile * 128 : tile * 128 + 128]
        if tile < 3:
            turned = part * cos_rows - swap_halves(part) * sin_rows
            part = turned if tile < 2 else jnp.where(low_lane, turned, part)
        key_value[:, tile * 128 : tile * 128 + 128] = part.astype(BF)
    grad_normed = dot_nt(grad_query[...], columns(whole, C_Q, DP)) + dot_nt(
        key_value[...], columns(whole, C_KV, 640)
    )
    through, grad_gain = norm_backward(entering[...].astype(F32), gains[0:1, :], grad_normed)
    grad_gains[0:1, :] = grad_gain
    through = through + grad_resid[...]

    @pl.when(is_first)
    def _():
        total[...] = through

    @pl.when(jnp.logical_not(is_first))
    def _():
        crossing[...] = through.astype(BF)
        grad_copy.start()

    for half in range(2):
        at = half * SUB
        here = slice(at, at + SUB)
        put(normed_one[...], grad_query[:, here], C_Q + at, SUB, (at, grad_gains[0:1, here]))
    put(normed_one[...], key_value[...], C_KV, 640)
    run("s1", 0, "go")
    run("s1", 2, "forward")
    run("s1", 1, "forward")
    run("s1", 0, "forward")
    put_ends(total[...])
    for group in (4, 3, 2):
        run("s1", group, "done")
    run("s2", 1, "go")
    run("s1", 1, "done")
    run("s1", 0, "done")
    run("s2", 0, "go")
    run("s2", 1, "forward")
    run("s2", 0, "done")
    run("s3", 0, "go")
    run("s2", 1, "done")
    run("s3", 1, "go")
    run("s3", 0, "done")
    run("s3", 1, "done")
    for slot, gain_result in enumerate((grad_gain_attn, grad_gain_mlp)):
        moved = pltpu.roll(grad_gains[2 + slot : 3 + slot, :], DP - me * PADDED, 1)
        gain_result[...] = moved[:, 0:SHARD]

    @pl.when(jnp.logical_not(is_first))
    def _():
        grad_copy.wait_send()

    for made in scatters:
        made.finish()


def rope_tables():
    frequency = BASE ** (-(np.arange(HD // 2, dtype=np.float32) * np.float32(2.0 / HD)))
    angles = np.arange(SEQ, dtype=np.float32)[:, None] * frequency[None, :].astype(np.float32)
    cos, sin = np.cos(angles), np.sin(angles)
    return (
        np.concatenate([cos, cos, cos, cos], axis=1).astype(np.float32),
        np.concatenate([-sin, sin, -sin, sin], axis=1).astype(np.float32),
    )


def hand_on(*refs):
    count = len(refs) // 2
    for source, target in zip(refs[:count], refs[count:]):
        target[...] = source[...]


def run_kernel(weights, gain_attn, gain_mlp, rows_in, lengths, cosine, sine):
    scratch = [
        ((RING, RING, RING, PADDED, C_ALL), BF),
        ((ROWS, DP), BF),
        ((ROWS, DP), BF),
        ((ROWS, DP), BF),
        ((D, DP), BF),
        ((ROWS, DP), BF),
        ((ROWS, DP), BF),
        ((ROWS, 640), BF),
        ((MICRO, KV, GROUP * SEQ, SEQ), F32),
        ((ROWS, DP), BF),
        ((ROWS, DP), F32),
        ((ROWS, DP), BF),
        ((ROWS, 2 * FF), BF),
        ((ROWS, FF), BF),
        ((ROWS, DP), F32),
        ((ROWS, DP), F32),
        ((ROWS, DP), F32),
        ((ROWS, DP), BF),
        ((ROWS, DP), BF),
        ((ROWS, 640), F32),
        ((8, DP), F32),
        ((8, DP), F32),
    ]
    scratch = [pltpu.VMEM(shape, kind) for shape, kind in scratch]
    scratch += [
        pltpu.SemaphoreType.DMA((SEMS,)),
        pltpu.SemaphoreType.DMA((2,)),
        pltpu.SemaphoreType.DMA((2,)),
        pltpu.SemaphoreType.REGULAR,
    ]
    scratch += [pltpu.VMEM(shape, BF) for shape in LANDS]
    vmem = pl.BlockSpec(memory_space=pltpu.VMEM)
    made = pl.pallas_call(
        kernel,
        out_shape=(
            jax.ShapeDtypeStruct((MICRO, D, SEQ), F32),
            *(
                jax.ShapeDtypeStruct((SHARD, 1, width), F32)
                for width in (D, 320, 320, D, FF, FF, FF)
            ),
            jax.ShapeDtypeStruct((1, SHARD), F32),
            jax.ShapeDtypeStruct((1, SHARD), F32),
        ),
        in_specs=[vmem] * 10 + [pl.BlockSpec(memory_space=pltpu.SMEM), vmem, vmem],
        out_specs=(vmem,) * 10,
        scratch_shapes=scratch,
        compiler_params=pltpu.CompilerParams(
            collective_id=0, has_side_effects=True, vmem_limit_bytes=64 * 1024 * 1024
        ),
    )(*weights, gain_attn, gain_mlp, rows_in, lengths, cosine, sine)
    count = len(made)
    return pl.pallas_call(
        hand_on,
        out_shape=tuple(jax.ShapeDtypeStruct(one.shape, one.dtype) for one in made),
        in_specs=[vmem] * count,
        out_specs=(vmem,) * count,
    )(*made)


def local(
    boundary, lengths, gain_attn, w_query, w_key, w_value, w_out, gain_mlp, w_gate, w_up, w_down
):
    cosine, sine = rope_tables()
    weights = (w_query[0], w_out[0].T, w_key[0], w_value[0], w_gate[0], w_up[0], w_down[0].T)
    ends, query, key, value, out, gate, up, down, gain_one, gain_two = run_kernel(
        weights,
        gain_attn,
        gain_mlp,
        boundary[0].transpose(0, 2, 1),
        lengths.T,
        jnp.asarray(cosine),
        jnp.asarray(sine),
    )

    def rows(grad):
        return grad.transpose(1, 0, 2)

    def turned(grad):
        return grad.transpose(1, 2, 0)

    return (
        ends.transpose(0, 2, 1)[None],
        gain_one,
        rows(query),
        rows(key),
        rows(value),
        turned(out),
        gain_two,
        rows(gate),
        rows(up),
        turned(down),
    )


def solution(mesh):
    row = P("section", "dp", None)
    column = P("section", None, "dp")
    gain = P("section", "dp")
    ends = P("section", None, "dp", None)
    weights = (gain, row, row, row, column, gain, row, row, column)
    return jax.shard_map(
        local,
        mesh=mesh,
        in_specs=(ends, P(None, "dp")) + weights,
        out_specs=(ends,) + weights,
        check_vma=False,
    )
```

time: 208 us -> 184 us (0.88)
  Pallas kernels: 200 us -> 183 us
  local copies, waits for them, and re-layouts: 7.1 us -> 0 us
    pallas_call x1, Pallas kernels: 200 us -> 181 us  [run_kernel(): pl.pallas_call(kernel, out_shape=(jax.ShapeDtypeStruct((MICRO, D, SEQ), F...]
    transpose x3 -> x0, local copies, waits for them, and re-layouts: 4.97 us -> none  [the longest x2 3.44 us: turned(): return result[:SHARD, :, first:first + count].transpose(1, 2, 0)]
    pallas_call x0 -> x1, Pallas kernels: none -> 2.64 us  [run_kernel(): pl.pallas_call(hand_on, out_shape=tuple((jax.ShapeDtypeStruct(one.shape,...]
where the time goes in v3:
time: 184 us
  Pallas kernels  183 us (99%)
    pallas_call x1, Pallas kernels, run_kernel(): pl.pallas_call(kernel, out_shape=(jax.ShapeDtypeStruct((MICRO, D, SEQ), F...  181 us

profile of v3, /device:TPU:0, one launch (start us, length us, event | category | flops | bytes accessed | tf_op | source)
XLA Modules:
  0.0 184.2 jit_solution(4780942864949074577)
XLA Ops:
  0.6 180.7 %shard_map.204 = (f32[2,960,128]{2,1,0:T(8,128)}, f32[15,1,960]{2,1,0:T(1,128)}, f32[15,1,320]{2,1,0:T(1,128)}, f32[15,1,320]{2,1,0:T(1,128)}, f32[15,1,960]{2,1...) custom-call(bf16[15,960]{1,0:T(8,128)(2,1)} %bitcast.29, ...), custom_call_target="tpu_custom_call" | custom-call | tf_op jit(solution)/shard_map/pallas_call | solution.py:835
  181.4 2.6 %shard_map.205 = (f32[2,960,128]{2,1,0:T(8,128)}, f32[15,1,960]{2,1,0:T(1,128)}, f32[15,1,320]{2,1,0:T(1,128)}, f32[15,1,320]{2,1,0:T(1,128)}, f32[15,1,960]{2,1...) custom-call(f32[2,960,128]{2,1,0:T(8,128)} %get-tuple-element.30.ref, ...), custom_call_target="tpu_custom_call" | custom-call | tf_op jit(solution)/shard_map/pallas_call | solution.py:854

commit v4 on v3

--- a/solution.py
+++ b/solution.py
@@ -456,7 +456,6 @@
         kind: [[make(entry) for entry in group] for group in groups]
         for kind, groups in PLAN.items()
     }
-    gathers = [made for made in started if isinstance(made, (DirectGather, RingGather))]
     scatters = [made for made in started if isinstance(made, (DirectScatter, RingScatter))]
 
     def run(kind, group, act):
@@ -608,30 +607,6 @@
         first, last = CHUNKS[chunk]
         lax.fori_loop(first // SUB, last // SUB, one, 0)
 
-    for chunk in range(len(CHUNKS)):
-        run("g3", chunk + 2, "done")
-        feed(chunk)
-
-    def put_ends(value):
-        high = value.astype(BF)
-        low = (value - high.astype(F32)).astype(BF)
-        for micro in range(MICRO):
-            rows = slice(micro * SEQ, micro * SEQ + SEQ)
-            ends[micro] = dot_nt(spread[...], high[rows]) + dot_nt(spread[...], low[rows])
-
-    @pl.when(is_first)
-    def _():
-        crossing[...] = total[...].astype(BF)
-        middle_copy.start()
-
-    for made in gathers:
-        made.finish()
-
-    @pl.when(is_first)
-    def _():
-        middle_copy.wait_send()
-        grad_copy.wait_recv()
-
     def put(left, right, first, count, gain=None):
         grad = dot_tn(left, right)
         if gain is not None:
@@ -641,8 +616,6 @@
             own = (row % PADDED == SHARD) & (row // PADDED == column // PADDED)
             grad = jnp.where(own, gain_row, grad)
         whole[:, :, :, :, pl.ds(first, count)] = grad.astype(BF).reshape(4, 4, 4, PADDED, count)
-
-    total_back[...] = jnp.zeros_like(total_back)
 
     def feed_back(chunk):
         def one(step, carry):
@@ -666,12 +639,47 @@
         first, last = CHUNKS[chunk]
         lax.fori_loop(first // SUB, last // SUB, one, 0)
 
-    feed_back(2)
-    run("s1", 4, "go")
-    feed_back(1)
-    run("s1", 3, "go")
-    feed_back(0)
-    run("s1", 2, "go")
+    def turn_back(chunk):
+        feed_back(chunk)
+        run("s1", chunk + 2, "go")
+
+    total_back[...] = jnp.zeros_like(total_back)
+    run("g1", 1, "finish")
+    run("g2", 1, "finish")
+    for chunk in range(len(CHUNKS)):
+        run("g3", chunk + 2, "done")
+        run("g3", chunk + 2, "finish")
+        feed(chunk)
+
+        @pl.when(jnp.logical_not(is_first))
+        def _():
+            turn_back(chunk)
+
+
+    def put_ends(value):
+        high = value.astype(BF)
+        low = (value - high.astype(F32)).astype(BF)
+        for micro in range(MICRO):
+            rows = slice(micro * SEQ, micro * SEQ + SEQ)
+            ends[micro] = dot_nt(spread[...], high[rows]) + dot_nt(spread[...], low[rows])
+
+    @pl.when(is_first)
+    def _():
+        crossing[...] = total[...].astype(BF)
+        middle_copy.start()
+
+    for kind, group in (("g1", 0), ("g2", 0), ("g3", 0), ("g3", 1)):
+        run(kind, group, "finish")
+
+    @pl.when(is_first)
+    def _():
+        middle_copy.wait_send()
+        grad_copy.wait_recv()
+
+    @pl.when(is_first)
+    def _():
+        for chunk in range(len(CHUNKS)):
+            turn_back(chunk)
 
     through, grad_gain = norm_backward(resid[...], gains[1:2, :], total_back[...])
     grad_gains[1:2, :] = grad_gain
@@ -684,7 +692,7 @@
         here = slice(at, at + SUB)
         put(grad_branch[...], mixed[:, here], C_O + at, SUB, (at, grad_gains[1:2, here]))
     run("s1", 1, "go")
-    run("s1", 4, "forward")
+    run("s1", 2, "forward")
 
     def attend_back(seq, carry):
         rows = pl.ds(pl.multiple_of(seq * SEQ, SEQ), SEQ)
@@ -753,11 +761,11 @@
         put(normed_one[...], grad_query[:, here], C_Q + at, SUB, (at, grad_gains[0:1, here]))
     put(normed_one[...], key_value[...], C_KV, 640)
     run("s1", 0, "go")
-    run("s1", 2, "forward")
+    run("s1", 4, "forward")
     run("s1", 1, "forward")
     run("s1", 0, "forward")
     put_ends(total[...])
-    for group in (4, 3, 2):
+    for group in (2, 3, 4):
         run("s1", group, "done")
     run("s2", 1, "go")
     run("s1", 1, "done")

time: 184 us -> 182 us (0.989)
  Pallas kernels: 183 us -> 181 us
    pallas_call x1, Pallas kernels: 181 us -> 178 us  [run_kernel(): pl.pallas_call(kernel, out_shape=(jax.ShapeDtypeStruct((MICRO, D, SEQ), F...]
where the time goes in v4:
time: 182 us
  Pallas kernels  181 us (99%)
    pallas_call x1, Pallas kernels, run_kernel(): pl.pallas_call(kernel, out_shape=(jax.ShapeDtypeStruct((MICRO, D, SEQ), F...  178 us

profile of v4, /device:TPU:0, one launch (start us, length us, event | category | flops | bytes accessed | tf_op | source)
XLA Modules:
  0.0 181.6 jit_solution(11074084214936327416)
XLA Ops:
  0.6 178.1 %shard_map.204 = (f32[2,960,128]{2,1,0:T(8,128)}, f32[15,1,960]{2,1,0:T(1,128)}, f32[15,1,320]{2,1,0:T(1,128)}, f32[15,1,320]{2,1,0:T(1,128)}, f32[15,1,960]{2,1...) custom-call(bf16[15,960]{1,0:T(8,128)(2,1)} %bitcast.29, ...), custom_call_target="tpu_custom_call" | custom-call | tf_op jit(solution)/shard_map/pallas_call | solution.py:843
  178.8 2.6 %shard_map.205 = (f32[2,960,128]{2,1,0:T(8,128)}, f32[15,1,960]{2,1,0:T(1,128)}, f32[15,1,320]{2,1,0:T(1,128)}, f32[15,1,320]{2,1,0:T(1,128)}, f32[15,1,960]{2,1...) custom-call(f32[2,960,128]{2,1,0:T(8,128)} %get-tuple-element.30.ref, ...), custom_call_target="tpu_custom_call" | custom-call | tf_op jit(solution)/shard_map/pallas_call | solution.py:862

commit v5 on v4

--- a/solution.py
+++ b/solution.py
@@ -692,7 +692,11 @@
         here = slice(at, at + SUB)
         put(grad_branch[...], mixed[:, here], C_O + at, SUB, (at, grad_gains[1:2, here]))
     run("s1", 1, "go")
-    run("s1", 2, "forward")
+
+    @pl.when(jnp.logical_not(is_first))
+    def _():
+        run("s1", 2, "forward")
+
 
     def attend_back(seq, carry):
         rows = pl.ds(pl.multiple_of(seq * SEQ, SEQ), SEQ)
@@ -726,7 +730,11 @@
         return carry
 
     lax.fori_loop(0, MICRO, attend_back, 0)
-    run("s1", 3, "forward")
+
+    @pl.when(jnp.logical_not(is_first))
+    def _():
+        run("s1", 3, "forward")
+
     grad_query = grad_mixed
     for tile in range(8):
         part = total_back[:, tile * 128 : tile * 128 + 128]
@@ -761,6 +769,12 @@
         put(normed_one[...], grad_query[:, here], C_Q + at, SUB, (at, grad_gains[0:1, here]))
     put(normed_one[...], key_value[...], C_KV, 640)
     run("s1", 0, "go")
+
+    @pl.when(is_first)
+    def _():
+        run("s1", 2, "forward")
+        run("s1", 3, "forward")
+
     run("s1", 4, "forward")
     run("s1", 1, "forward")
     run("s1", 0, "forward")

time: 182 us -> 181 us (level)
  no operation moved by 1% of the time
where the time goes in v5:
time: 181 us
  Pallas kernels  180 us (99%)
    pallas_call x1, Pallas kernels, run_kernel(): pl.pallas_call(kernel, out_shape=(jax.ShapeDtypeStruct((MICRO, D, SEQ), F...  178 us

profile of v5, /device:TPU:0, one launch (start us, length us, event | category | flops | bytes accessed | tf_op | source)
XLA Modules:
  0.0 181.2 jit_solution(17441496628667407548)
XLA Ops:
  0.6 177.8 %shard_map.204 = (f32[2,960,128]{2,1,0:T(8,128)}, f32[15,1,960]{2,1,0:T(1,128)}, f32[15,1,320]{2,1,0:T(1,128)}, f32[15,1,320]{2,1,0:T(1,128)}, f32[15,1,960]{2,1...) custom-call(bf16[15,960]{1,0:T(8,128)(2,1)} %bitcast.29, ...), custom_call_target="tpu_custom_call" | custom-call | tf_op jit(solution)/shard_map/pallas_call | solution.py:857
  178.4 2.6 %shard_map.205 = (f32[2,960,128]{2,1,0:T(8,128)}, f32[15,1,960]{2,1,0:T(1,128)}, f32[15,1,320]{2,1,0:T(1,128)}, f32[15,1,320]{2,1,0:T(1,128)}, f32[15,1,960]{2,1...) custom-call(f32[2,960,128]{2,1,0:T(8,128)} %get-tuple-element.30.ref, ...), custom_call_target="tpu_custom_call" | custom-call | tf_op jit(solution)/shard_map/pallas_call | solution.py:876
